TPU v7x, 128 devices: a whole 4x4x4 slice. The times are simulated.
128 devices in a mesh: gx: 16 (over z, y_hi, core), gy: 8 (over x, y_lo).
Axes of the slice: x: 4, y: 4 (y_hi: 2, y_lo: 2; y = y_hi * 2 + y_lo), z: 4, core: 2. Of those that a mesh axis runs over, the one named last changes fastest.
Arguments:
- residents: float32 [16, 64, 32768], P(None, 'gx', 'gy'), as said below
- cell_count: int32 [64, 8192], P('gx', 'gy'), may hold values from 0 to 4, as said below
- outbox: float32 [16, 64, 2048], P(None, 'gx', 'gy'), as said below
- corner_box: float32 [16, 64, 512], P(None, 'gx', 'gy'), as said below
- face_cell: int32 [64, 2048], P('gx', 'gy'), may hold values from 0 to 4095, as said below
- corner_cell: int32 [64, 512], P('gx', 'gy'), may hold values from 0 to 4095, as said below
- mig_count: int32 [128, 8], P('gx', 'gy'), may hold values from 0 to 256, as said below
Outputs:
- resident_next: float32 [16, 64, 32768], P(None, 'gx', 'gy')
- migrant_next: float32 [16, 64, 2048], P(None, 'gx', 'gy')
- corner_next: float32 [16, 64, 512], P(None, 'gx', 'gy')
Inputs may be any that keep to these rules, and one draw needn't show every extreme that they name: `residents`: rows 0 to 2 lie in [-0.5, 0.5) and row 15 is positive. `outbox`: rows 0 to 2 lie in [-0.5, 0.5) and row 15 is positive. `corner_box`: rows 0 to 2 lie in [-0.5, 0.5) and row 15 is positive. `cell_count`: cells with z = 0 or z = 63 hold no particle; some cell holds 4. `face_cell`: A migrant's cell lies on the face of the receiving tile through which it enters (x = 0 when sx = 1, x = 3 when sx = -1, likewise y), with 1 <= z <= 62. `corner_cell`: A diagonal migrant's cell lies on the corner column of the receiving tile through which it enters, with 1 <= z <= 62. `mig_count`: face directions count at most 256 and diagonal ones at most 64; some tile sends 256 toward some face direction and some tile sends 64 toward some diagonal direction.
All inputs are finite; a program needn't handle non-finite values.
Results may differ from a plain program's by a relative error of at most 0.0003.
Values sent between devices are 32-bit elements; how exact they have to be, the bound alone decides.
No kernel may reach another device: no remote copies, remote signals or barrier semaphores. Data moves between devices by JAX's collectives and lax.ppermute only.
A program may use at most 128 MiB of HBM per device.

v0:
```python
import jax
import jax.numpy as jnp
from jax import lax
from jax.experimental import pallas as pl
from jax.experimental.pallas import tpu as pltpu
from jax.sharding import PartitionSpec as P

CX = 4
CY = 16
NZ = 64
MIG = 256
CORNER = 64
PAIR = 2 * CORNER
WIDE = MIG + PAIR
YY = 20
YP = 24
Y_ROWS = 104
X_ROWS = 168
X_STATES = 112
time_step = 0.1
gravity = 1.0
mass_floor = 0.5
STEPS = (-1, 0, 1)
F32 = jnp.float32
BF16 = jnp.bfloat16


def spline(offset):
    low = 0.5 - offset
    high = 0.5 + offset
    return (0.5 * (low * low), 0.75 - offset * offset, 0.5 * (high * high))


def deposit_terms(state, living):
    mass = state[15] * living
    affine = [mass * state[6 + j] for j in range(9)]
    carried = []
    for i in range(3):
        skew = affine[3 * i] * state[0] + affine[3 * i + 1] * state[1] + affine[3 * i + 2] * state[2]
        carried.append(mass * state[3 + i] - skew)
    return mass, carried, affine


def placed(rows, width, cell, weights, wrap=None):
    row = lax.broadcasted_iota(jnp.int32, (rows, width), 0)
    step = row - cell
    if wrap is not None:
        step = jnp.where(step > wrap // 2, step - wrap, jnp.where(step < -wrap // 2, step + wrap, step))
    low, mid, high = weights
    zero = jnp.zeros((rows, width), F32)
    is_low, is_high = step == -1, step == 1
    moment = jnp.where(is_low, -low, jnp.where(is_high, high, zero))
    plain = jnp.where(is_low, low, jnp.where(is_high, high, jnp.where(step == 0, mid, zero)))
    return plain, moment


def split(value):
    coarse = value.astype(BF16)
    fine = (value - coarse.astype(F32)).astype(BF16)
    return coarse, fine


def low_half(shape):
    return lax.broadcasted_iota(jnp.int32, shape, len(shape) - 1) % 128 < NZ


def swap_half(value):
    return pltpu.roll(value, NZ, value.ndim - 1)


def scatter_product(lhs, depth_plain, depth_moment):
    rhs = jnp.concatenate([depth_plain, depth_moment], axis=1)
    rhs = jnp.concatenate(split(rhs), axis=0)
    coarse, fine = split(lhs)
    dims = (((1,), (1,)), ((), ()))
    return lax.dot_general(coarse, rhs, dims, preferred_element_type=F32) + lax.dot_general(
        fine, rhs, dims, preferred_element_type=F32
    )


def row_of(value, g):
    return value[g : g + 1, :]


def join_pairs(value, first, second):
    return jnp.concatenate([value[first : first + 1, :], value[second : second + 1, :]], axis=1)


def fold_pair(first, second):
    low = low_half(first.shape)
    return jnp.where(low, first, second) + swap_half(jnp.where(low, second, first))


def resident_living(count_ref, y):
    lane = 128 * (y // 2)
    counts = count_ref[:, lane : lane + 128]
    low = low_half(counts.shape)
    if y % 2 == 0:
        counts = jnp.where(low, counts, swap_half(counts))
    else:
        counts = jnp.where(low, swap_half(counts), counts)
    counts = jnp.concatenate([counts, counts], axis=0)
    row = lax.broadcasted_iota(jnp.int32, (8, 128), 0)
    lane_id = lax.broadcasted_iota(jnp.int32, (8, 128), 1)
    slot = 2 * (row // CX) + lane_id // NZ
    return (slot < counts).astype(F32)


def deposit_residents(res_ref, count_ref, terms_ref, total_ref, first, last):
    row = lax.broadcasted_iota(jnp.int32, (8, 128), 0)
    keep = row < CX
    for y in range(first, last):
        state = [res_ref[c, y] for c in range(16)]
        mass, carried, affine = deposit_terms(state, resident_living(count_ref, y))
        stored = [mass] + carried + affine
        for axis in range(3):
            stored += list(spline(state[axis]))
        for k, value in enumerate(stored):
            terms_ref[y, k] = value
    for ex in STEPS:
        sums = {}

        def finish_node(node):
            for c in range(4):
                value = (
                    sums.pop((node, c, 0))
                    + pltpu.roll(sums.pop((node, c, 1)), 1, 1)
                    + pltpu.roll(sums.pop((node, c, -1)), 127, 1)
                )
                value = jnp.where(keep, value + pltpu.roll(value, CX, 0), 0.0)
                if ex != 0:
                    value = pltpu.roll(value, ex % 8, 0)
                at = (node + 2) * 8
                total_ref[c, at : at + 8, :] += value

        for y in range(first, last):
            term = [terms_ref[y, k] for k in range(13)]
            weight_x = terms_ref[y, 13 + ex + 1]
            weight_y = [terms_ref[y, 16 + k] for k in range(3)]
            along = [term[0]]
            for i in range(3):
                value = term[1 + i]
                if ex != 0:
                    value = value + term[4 + 3 * i] if ex > 0 else value - term[4 + 3 * i]
                along.append(value)
            for ez in STEPS:
                weight = weight_x * terms_ref[y, 19 + ez + 1]
                for c in range(4):
                    value = along[c]
                    if c > 0 and ez != 0:
                        lift = term[4 + 3 * (c - 1) + 2]
                        value = value + lift if ez > 0 else value - lift
                    value = weight * value
                    parts = [value, value, value]
                    if c > 0:
                        lean = weight * term[4 + 3 * (c - 1) + 1]
                        parts = [value - lean, value, value + lean]
                    for ey in STEPS:
                        key = (y + ey, c, ez)
                        part = weight_y[ey + 1] * parts[ey + 1]
                        sums[key] = sums[key] + part if key in sums else part
            finish_node(y - 1)
        finish_node(last - 1)
        finish_node(last)


def edge_kernel(count_ref, res_ref, cells_ref, outbox_ref, corner_ref, face_cell_ref, corner_cell_ref,
                msg0_ref, msg1_ref, ahead_ref, total_ref, terms_ref, stage_ref):
    total_ref[...] = jnp.zeros_like(total_ref)

    def living_of(width, offset):
        slot = lax.broadcasted_iota(jnp.int32, (4, width), 1)
        row = lax.broadcasted_iota(jnp.int32, (4, width), 0)
        counts = jnp.where(
            row < 2,
            jnp.where(row == 0, count_ref[offset], count_ref[offset + 1]),
            jnp.where(row == 2, count_ref[offset + 2], count_ref[offset + 3]),
        )
        return slot < counts

    face_cells = jnp.where(living_of(MIG, 0), face_cell_ref[...], -1).astype(F32)
    corner_cells = jnp.where(living_of(CORNER, 4), corner_cell_ref[...], -1).astype(F32)

    faces = [outbox_ref[c] for c in range(16)]
    corners = [corner_ref[c] for c in range(16)]

    for c, (face, corner) in enumerate(zip(faces + [face_cells], corners + [corner_cells])):
        for side in range(2):
            pair = join_pairs(corner, side, side + 2)
            if c < 16:
                stage_ref[side, 48 + c : 49 + c, :] = face[2 + side : 3 + side, 0:128]
                stage_ref[side, 64 + c : 65 + c, :] = face[2 + side : 3 + side, 128:256]
                stage_ref[side, 80 + c : 81 + c, :] = pair
                ahead_ref[side, c : c + 1, :] = face[side : side + 1, 0:128]
                ahead_ref[side, 16 + c : 17 + c, :] = face[side : side + 1, 128:256]
            else:
                stage_ref[side, 96:97, :] = face[2 + side : 3 + side, 0:128]
                stage_ref[side, 97:98, :] = face[2 + side : 3 + side, 128:256]
                stage_ref[side, 98:99, :] = pair
                stage_ref[side, 99:104, :] = jnp.zeros((5, 128), F32)
                ahead_ref[side, 32:33, :] = face[side : side + 1, 0:128]
                ahead_ref[side, 33:34, :] = face[side : side + 1, 128:256]
                ahead_ref[side, 34:40, :] = jnp.zeros((6, 128), F32)

    def decode(cells):
        number = cells.astype(jnp.int32)
        living = (number >= 0).astype(F32)
        return living, number // (CY * NZ), (number // NZ) % CY, number % NZ

    def wide(face, corner):
        pairs = jnp.concatenate([join_pairs(corner, 0, 1), join_pairs(corner, 2, 3)], axis=0)
        return jnp.concatenate([face[0:2, :], pairs], axis=1)

    state = [wide(faces[c], corners[c]) for c in range(16)]
    living, _, cell_y, cell_z = decode(wide(face_cells, corner_cells))
    lane = lax.broadcasted_iota(jnp.int32, (2, WIDE), 1)
    cell_y = cell_y + jnp.where(lane < MIG, 2, jnp.where(lane < MIG + CORNER, 2 + CY, 2 - CY))
    mass, carried, affine = deposit_terms(state, living)
    weights = [spline(state[axis]) for axis in range(3)]
    for g in range(2):
        depth = placed(NZ, WIDE, row_of(cell_z, g), [row_of(w, g) for w in weights[2]])
        across, across_moment = placed(YP, WIDE, row_of(cell_y, g), [row_of(w, g) for w in weights[1]])
        lines = []
        zero = jnp.zeros((YP, WIDE), F32)
        for c in range(4):
            for e in STEPS:
                weight = row_of(weights[0][e + 1], g)
                if c == 0:
                    plain, moment = (weight * row_of(mass, g)) * across, zero
                else:
                    base = row_of(carried[c - 1], g) + e * row_of(affine[3 * (c - 1)], g)
                    plain = (weight * base) * across + (
                        weight * row_of(affine[3 * (c - 1) + 1], g)
                    ) * across_moment
                    moment = (weight * row_of(affine[3 * (c - 1) + 2], g)) * across
                lines.append(jnp.concatenate([plain, moment], axis=1))
        product = scatter_product(jnp.concatenate(lines, axis=0), *depth)
        for c in range(4):
            for e in STEPS:
                row = ((CX if g == 0 else -1) + e) % 8
                at = (3 * c + e + 1) * YP
                total_ref[c, pl.ds(row, YP, stride=8), :] += product[at : at + YP, :]

    state = [face[2:4, :] for face in faces]
    living, cell_x, _, cell_z = decode(face_cells[2:4, :])
    mass, carried, affine = deposit_terms(state, living)
    weights = [spline(state[axis]) for axis in range(3)]
    for g in range(2):
        depth = placed(NZ, MIG, row_of(cell_z, g), [row_of(w, g) for w in weights[2]])
        across, across_moment = placed(8, MIG, row_of(cell_x, g), [row_of(w, g) for w in weights[0]], 8)
        lines = []
        zero = jnp.zeros((8, MIG), F32)
        for c in range(4):
            for e in STEPS:
                weight = row_of(weights[1][e + 1], g)
                if c == 0:
                    plain, moment = (weight * row_of(mass, g)) * across, zero
                else:
                    base = row_of(carried[c - 1], g) + e * row_of(affine[3 * (c - 1) + 1], g)
                    plain = (weight * base) * across + (
                        weight * row_of(affine[3 * (c - 1)], g)
                    ) * across_moment
                    moment = (weight * row_of(affine[3 * (c - 1) + 2], g)) * across
                lines.append(jnp.concatenate([plain, moment], axis=1))
        product = scatter_product(jnp.concatenate(lines, axis=0), *depth)
        for c in range(4):
            for e in STEPS:
                at = ((CY if g == 0 else -1) + e + 2) * 8
                line = (3 * c + e + 1) * 8
                total_ref[c, at : at + 8, :] += product[line : line + 8, :]

    deposit_residents(res_ref, cells_ref, terms_ref, total_ref, 0, 2)
    deposit_residents(res_ref, cells_ref, terms_ref, total_ref, CY - 2, CY)

    for side in range(2):
        for pair in range(2):
            for j in range(3):
                at = ((CY + 1 + j) if side == 0 else j) * 8
                stage_ref[side, (3 * pair + j) * 8 : (3 * pair + j + 1) * 8, :] = fold_pair(
                    total_ref[2 * pair, at : at + 8, :], total_ref[2 * pair + 1, at : at + 8, :]
                )
    parity = lax.axis_index("gy") % 2
    msg0_ref[...] = stage_ref[parity]
    msg1_ref[...] = stage_ref[1 - parity]


def inner_kernel(res_ref, cells_ref, before_ref, grid_ref, total_ref, terms_ref):
    total_ref[...] = before_ref[...]
    deposit_residents(res_ref, cells_ref, terms_ref, total_ref, 2, CY - 2)
    for pair in range(2):
        for yy in range(YY):
            at = yy * 8
            grid_ref[pair, at : at + 8, :] = fold_pair(
                total_ref[2 * pair, at : at + 8, :], total_ref[2 * pair + 1, at : at + 8, :]
            )


def turn_kernel(grid_ref, in0_ref, in1_ref, ahead_ref, joined_ref, msg0_ref, msg1_ref, got_ref, stage_ref):
    parity = lax.axis_index("gy") % 2
    got_ref[parity] = in1_ref[...]
    got_ref[1 - parity] = in0_ref[...]
    joined_ref[...] = grid_ref[...]
    for pair in range(2):
        for j in range(3):
            line = (3 * pair + j) * 8
            for side, yy in ((0, 1 + j), (1, CY + j)):
                joined_ref[pair, yy * 8 : yy * 8 + 8, :] += got_ref[side, line : line + 8, :]
    low = low_half((16, 128))
    for side in range(2):
        for pair in range(2):
            for j in range(3):
                row = (3 + j) if side == 0 else (6 + j) % 8
                at = (3 * pair + j) * 18
                stage_ref[side, at : at + 18, :] = joined_ref[pair, pl.ds(8 + row, 18, stride=8), :]
        stage_ref[side, 108:112, :] = jnp.zeros((4, 128), F32)
        stage_ref[side, X_STATES : X_STATES + 32, :] = ahead_ref[side, 0:32, :]
        from_below, from_above = got_ref[0, 80:96, :], got_ref[1, 80:96, :]
        cell_below, cell_above = got_ref[0, 96:104, :], got_ref[1, 96:104, :]
        if side == 0:
            states = jnp.where(low, from_below, swap_half(from_above))
            cells = jnp.where(low[0:8], cell_below, swap_half(cell_above))
        else:
            states = jnp.where(low, swap_half(from_below), from_above)
            cells = jnp.where(low[0:8], swap_half(cell_below), cell_above)
        stage_ref[side, X_STATES + 32 : X_STATES + 48, :] = states
        stage_ref[side, X_STATES + 48 : X_STATES + 56, :] = jnp.zeros((8, 128), F32)
        stage_ref[side, X_STATES + 48 : X_STATES + 50, :] = ahead_ref[side, 32:34, :]
        stage_ref[side, X_STATES + 50 : X_STATES + 51, :] = cells[2:3, :]
    parity = lax.axis_index("gx") % 2
    msg0_ref[...] = stage_ref[parity]
    msg1_ref[...] = stage_ref[1 - parity]


def gather_product(nodes, depth_plain, depth_moment):
    low = low_half(nodes.shape)
    coarse = nodes.astype(BF16).astype(F32)
    lhs = jnp.where(low, coarse, nodes - coarse).astype(BF16)
    rhs = jnp.concatenate([depth_plain, depth_moment], axis=1)
    coarse, fine = split(rhs)
    dims = (((1,), (0,)), ((), ()))
    return lax.dot_general(
        lhs, jnp.concatenate([coarse, coarse], axis=0), dims, preferred_element_type=F32
    ) + lax.dot_general(lhs, jnp.concatenate([fine, fine], axis=0), dims, preferred_element_type=F32)


def contract(product, rows, width, normal, across, across_moment, normal_axis, across_axis):
    velocity, slopes = [], []
    for i in range(3):
        plain = [product[(3 * i + k) * rows : (3 * i + k + 1) * rows, 0:width] for k in range(3)]
        lifted = [
            product[(3 * i + k) * rows : (3 * i + k + 1) * rows, width : 2 * width] for k in range(3)
        ]
        low, mid, high = [normal[k] * plain[k] for k in range(3)]
        summed = low + mid + high
        stepped = high - low
        raised = normal[0] * lifted[0] + normal[1] * lifted[1] + normal[2] * lifted[2]
        velocity.append(jnp.sum(across * summed, axis=0, keepdims=True))
        slope = [None, None, jnp.sum(across * raised, axis=0, keepdims=True)]
        slope[normal_axis] = jnp.sum(across * stepped, axis=0, keepdims=True)
        slope[across_axis] = jnp.sum(across_moment * summed, axis=0, keepdims=True)
        slopes.append(slope)
    return velocity, slopes


def finished(state, living, velocity, slopes):
    out = [living * (state[k] + time_step * velocity[k]) for k in range(3)]
    out += [living * velocity[k] for k in range(3)]
    for i in range(3):
        out += [living * (4.0 * (slopes[i][k] - state[k] * velocity[i])) for k in range(3)]
    return out + [living * state[15]]


def last_kernel(res_ref, cells_ref, joined_ref, y0_ref, y1_ref, x0_ref, x1_ref,
                out_ref, face_out_ref, corner_out_ref, got_y_ref, got_x_ref, grid_ref, vel_ref, near_ref):
    parity = lax.axis_index("gy") % 2
    got_y_ref[parity] = y1_ref[...]
    got_y_ref[1 - parity] = y0_ref[...]
    parity = lax.axis_index("gx") % 2
    got_x_ref[parity] = x1_ref[...]
    got_x_ref[1 - parity] = x0_ref[...]

    grid_ref[...] = joined_ref[...]
    for side in range(2):
        for pair in range(2):
            for j in range(3):
                row = ((3 + j) if side == 0 else (6 + j) % 8) ^ 4
                at = (3 * pair + j) * 18
                grid_ref[pair, pl.ds(8 + row, 18, stride=8), :] += got_x_ref[side, at : at + 18, :]

    vel_ref[...] = jnp.zeros_like(vel_ref)
    low = low_half((8, 128))
    row = lax.broadcasted_iota(jnp.int32, (8, 128), 0)
    layer = lax.broadcasted_iota(jnp.int32, (8, 128), 1) % NZ
    inside = (layer > 0) & (layer < NZ - 1)
    upper = row < CX
    for yy in range(1, CY + 3):
        first = grid_ref[0, yy * 8 : yy * 8 + 8, :]
        second = grid_ref[1, yy * 8 : yy * 8 + 8, :]
        first_swap, second_swap = swap_half(first), swap_half(second)
        mass = jnp.maximum(jnp.where(low, first, first_swap), mass_floor)
        momentum = (
            jnp.where(low, first_swap, first),
            jnp.where(low, second, second_swap),
            jnp.where(low, second_swap, second),
        )
        for i in range(3):
            value = momentum[i] / mass
            if i == 2:
                value = value - time_step * gravity
            value = jnp.where(inside, value, 0.0)
            vel_ref[i, yy * 8 : yy * 8 + 8, :] = value
            for ex in STEPS:
                near = jnp.where(
                    upper,
                    pltpu.roll(value, (-ex) % 8, 0) if ex != 0 else value,
                    pltpu.roll(value, (CX - ex) % 8, 0),
                )
                near_ref[ex + 1, 1, i, yy - 1] = near
                near_ref[ex + 1, 0, i, yy - 1] = pltpu.roll(near, 1, 1)
                near_ref[ex + 1, 2, i, yy - 1] = pltpu.roll(near, 127, 1)

    for side in range(2):
        def wide_row(k):
            return jnp.concatenate([got_x_ref[side, a : a + 1, :] for a in k], axis=1)

        base = X_STATES
        state = [wide_row((base + c, base + 16 + c, base + 32 + c)) for c in range(16)]
        number = wide_row((base + 48, base + 49, base + 50)).astype(jnp.int32)
        living = (number >= 0).astype(F32)
        weights = [spline(state[axis]) for axis in range(3)]
        depth = placed(NZ, WIDE, number % NZ, weights[2])
        across, across_moment = placed(YP, WIDE, (number // NZ) % CY + 2, weights[1])
        lines = []
        for i in range(3):
            for e in STEPS:
                at = ((0 if side == 0 else CX - 1) + e) % 8
                lines.append(vel_ref[i, pl.ds(at, YP, stride=8), :])
        product = gather_product(jnp.concatenate(lines, axis=0), *depth)
        velocity, slopes = contract(product, YP, WIDE, weights[0], across, across_moment, 0, 1)
        for c, value in enumerate(finished(state, living, velocity, slopes)):
            face_out_ref[c, side : side + 1, :] = value[:, 0:MIG]
            corner_out_ref[c, 2 * side : 2 * side + 1, :] = value[:, MIG : MIG + CORNER]
            corner_out_ref[c, 2 * side + 1 : 2 * side + 2, :] = value[:, MIG + CORNER : WIDE]

    for side in range(2):
        def face_row(k):
            return jnp.concatenate([got_y_ref[side, a : a + 1, :] for a in k], axis=1)

        state = [face_row((48 + c, 64 + c)) for c in range(16)]
        number = face_row((96, 97)).astype(jnp.int32)
        living = (number >= 0).astype(F32)
        weights = [spline(state[axis]) for axis in range(3)]
        depth = placed(NZ, MIG, number % NZ, weights[2])
        across, across_moment = placed(8, MIG, jnp.maximum(number, 0) // (CY * NZ), weights[0], 8)
        lines = []
        for i in range(3):
            for e in STEPS:
                at = ((0 if side == 0 else CY - 1) + 2 + e) * 8
                lines.append(vel_ref[i, at : at + 8, :])
        product = gather_product(jnp.concatenate(lines, axis=0), *depth)
        velocity, slopes = contract(product, 8, MIG, weights[1], across, across_moment, 1, 0)
        for c, value in enumerate(finished(state, living, velocity, slopes)):
            face_out_ref[c, 2 + side : 3 + side, :] = value

    for y in range(CY):
        state = [res_ref[c, y] for c in range(16)]
        living = resident_living(cells_ref, y)
        weights = [spline(state[axis]) for axis in range(3)]
        velocity, slopes = [], []
        for i in range(3):
            by_x = []
            for kx in range(3):
                by_y = []
                for ky in range(3):
                    low_z, mid_z, high_z = [
                        weights[2][kz] * near_ref[kx, kz, i, y + ky] for kz in range(3)
                    ]
                    by_y.append((low_z + mid_z + high_z, high_z - low_z))
                low_y, mid_y, high_y = [weights[1][k] * by_y[k][0] for k in range(3)]
                raised = (
                    weights[1][0] * by_y[0][1] + weights[1][1] * by_y[1][1] + weights[1][2] * by_y[2][1]
                )
                by_x.append((low_y + mid_y + high_y, high_y - low_y, raised))
            low_x, mid_x, high_x = [weights[0][k] * by_x[k][0] for k in range(3)]
            velocity.append(low_x + mid_x + high_x)
            slope = [high_x - low_x]
            for part in (1, 2):
                slope.append(
                    weights[0][0] * by_x[0][part]
                    + weights[0][1] * by_x[1][part]
                    + weights[0][2] * by_x[2][part]
                )
            slopes.append(slope)
        for c, value in enumerate(finished(state, living, velocity, slopes)):
            out_ref[c, y] = value


def partner(index, phase, count):
    return (((index - phase) % count ^ 1) + phase) % count


def swapped(value, axis, phase):
    count = lax.axis_size(axis)
    return lax.ppermute(value, axis, [(i, partner(i, phase, count)) for i in range(count)])


VMEM = pl.BlockSpec(memory_space=pltpu.VMEM)
SMEM = pl.BlockSpec(memory_space=pltpu.SMEM)


def call(kernel, in_specs, out_shapes, scratch, flops):
    return pl.pallas_call(
        kernel,
        in_specs=in_specs,
        out_specs=[VMEM] * len(out_shapes),
        out_shape=[jax.ShapeDtypeStruct(shape, F32) for shape in out_shapes],
        scratch_shapes=[pltpu.VMEM(shape, F32) for shape in scratch],
        compiler_params=pltpu.CompilerParams(vmem_limit_bytes=24 * 1024 * 1024),
        cost_estimate=pl.CostEstimate(flops=flops, bytes_accessed=1 << 20, transcendentals=0),
    )


def body(residents, cell_count, outbox, corner_box, face_cell, corner_cell, mig_count):
    res = residents.reshape(16, CX, CY, 2, 128).transpose(0, 2, 3, 1, 4).reshape(16, CY, 8, 128)
    msg0, msg1, ahead, total = call(
        edge_kernel,
        [SMEM] + [VMEM] * 6,
        [(Y_ROWS, 128), (Y_ROWS, 128), (2, 40, 128), (4, YP * 8, 128)],
        [(CY, 22, 8, 128), (2, Y_ROWS, 128)],
        10_000_000,
    )(mig_count.reshape(8), res, cell_count, outbox, corner_box, face_cell, corner_cell)
    y1 = swapped(msg1, "gy", 1)
    y0 = swapped(msg0, "gy", 0)
    (grid,) = call(
        inner_kernel, [VMEM] * 3, [(2, YY * 8, 128)], [(4, YP * 8, 128), (CY, 22, 8, 128)], 10_000_000
    )(res, cell_count, total)
    joined, msg0, msg1 = call(
        turn_kernel,
        [VMEM] * 4,
        [(2, YY * 8, 128), (X_ROWS, 128), (X_ROWS, 128)],
        [(2, Y_ROWS, 128), (2, X_ROWS, 128)],
        1_000_000,
    )(grid, y0, y1, ahead)
    x1 = swapped(msg1, "gx", 1)
    x0 = swapped(msg0, "gx", 0)
    out, face_out, corner_out = call(
        last_kernel,
        [VMEM] * 7,
        [(16, CY, 8, 128), (16, 4, MIG), (16, 4, CORNER)],
        [
            (2, Y_ROWS, 128),
            (2, X_ROWS, 128),
            (2, YY * 8, 128),
            (3, YP * 8, 128),
            (3, 3, 3, CY + 2, 8, 128),
        ],
        10_000_000,
    )(res, cell_count, joined, y0, y1, x0, x1)
    out = out.reshape(16, CY, 2, CX, 128).transpose(0, 3, 1, 2, 4).reshape(16, CX, CY * 256)
    return out, face_out, corner_out


def solution(mesh):
    in_specs = (
        P(None, "gx", "gy"),
        P("gx", "gy"),
        P(None, "gx", "gy"),
        P(None, "gx", "gy"),
        P("gx", "gy"),
        P("gx", "gy"),
        P("gx", "gy"),
    )
    out_specs = (P(None, "gx", "gy"), P(None, "gx", "gy"), P(None, "gx", "gy"))
    return jax.shard_map(body, mesh=mesh, in_specs=in_specs, out_specs=out_specs, check_vma=False)
```

profile of v0, /device:TPU:0, one launch (start us, length us, event | category | flops | bytes accessed | tf_op | source)
XLA Modules:
  0.0 27.1 jit_solution(5290647874002612411)
XLA Ops:
  0.6 0.0 copy-start.6
  0.6 0.0 copy-start.7
  0.7 0.7 %copy-done.6 = s32[4,64]{1,0:T(4,128)S(1)} copy-done((s32[4,64]{1,0:T(4,128)S(1)}, s32[4,64]{1,0:T(4,128)}, u32[]{:S(2)}) %copy-start.6) | copy-done | bytes 1048
  1.3 0.0 copy-done.7
  1.3 0.0 copy-start
  1.3 1.2 %copy-done = f32[16,4,4096]{2,1,0:T(4,128)S(1)} copy-done((f32[16,4,4096]{2,1,0:T(4,128)S(1)}, f32[16,4,4096]{2,1,0:T(4,128)}, u32[]{:S(2)}) %copy-start) | copy-done | bytes 1048600
  2.5 0.0 copy-start.2
  2.5 0.7 %copy-done.2 = s32[4,1024]{1,0:T(4,128)S(1)} copy-done((s32[4,1024]{1,0:T(4,128)S(1)}, s32[4,1024]{1,0:T(4,128)}, u32[]{:S(2)}) %copy-start.2) | copy-done | bytes 16408
  3.3 0.8 %copy-done.3 = f32[16,4,256]{2,1,0:T(4,128)S(1)} copy-done((f32[16,4,256]{2,1,0:T(4,128)S(1)}, f32[16,4,256]{2,1,0:T(4,128)}, u32[]{:S(2)}) %copy-start.3) | copy-done | bytes 65560
  4.1 0.8 %copy-done.4 = f32[16,4,64]{2,1,0:T(4,128)S(1)} copy-done((f32[16,4,64]{2,1,0:T(4,128)S(1)}, f32[16,4,64]{2,1,0:T(4,128)}, u32[]{:S(2)}) %copy-start.4) | copy-done | bytes 16408
  4.9 0.7 %copy-done.5 = s32[4,256]{1,0:T(4,128)S(1)} copy-done((s32[4,256]{1,0:T(4,128)S(1)}, s32[4,256]{1,0:T(4,128)}, u32[]{:S(2)}) %copy-start.5) | copy-done | bytes 4120
  5.5 1.9 %shard_map.94 = (f32[104,128]{1,0:T(8,128)S(1)}, f32[104,128]{1,0:T(8,128)S(1)}, f32[2,40,128]{2,1,0:T(8,128)S(1)}, f32[4,192,128]{2,1,0:T(8,128)S(1)}) custom-call(s32[8]{0:T(128)S(1)} %bitcast.14, f32[16,16,8,128]{3,2,1,0:T(8,128)S(1)} %bitcast.11, s32[4,1024]{1,0:T(4,128)S(1)} %copy-done.2, f32[16,4,256]{2,1,0:T(4,128)S(1)} %copy-done.3, ...), custom_call_target="tpu_custom_call" | custom-call | flops 10000000 | bytes 1048576 | tf_op jit(solution)/shard_map/pallas_call | solution.py:525
  7.5 1.7 %collective-permute-start = (f32[104,128]{1,0:T(8,128)S(1)}, f32[104,128]{1,0:T(8,128)S(1)}, u32[]{:S(2)}, u32[]{:S(2)}) collective-permute-start(f32[104,128]{1,0:T(8,128)S(1)} %get-tuple-element.14), channel_id=1, source_target_pairs={{0,1},{1,0},{2,3},{3,2},{4,5},{5,4},{6,7},{7,6},{8,9},{9,8},{10,11... | collective-permute-start | bytes 159752 | tf_op jit(solution)/shard_map/ppermute | solution.py:504
  9.2 2.6 %collective-permute-start.1 = (f32[104,128]{1,0:T(8,128)S(1)}, f32[104,128]{1,0:T(8,128)S(1)}, u32[]{:S(2)}, u32[]{:S(2)}) collective-permute-start(f32[104,128]{1,0:T(8,128)S(1)} %get-tuple-element.15), channel_id=1, source_target_pairs={{0,7},{1,2},{2,1},{3,4},{4,3},{5,6},{6,5},{7,0},{8,15},{9,10},{10,... | collective-permute-start | bytes 159752 | tf_op jit(solution)/shard_map/ppermute | solution.py:504
  11.9 0.0 copy-done.1
  11.9 1.0 %shard_map.95.grid_ref = f32[2,160,128]{2,1,0:T(8,128)S(1)} custom-call(f32[16,16,8,128]{3,2,1,0:T(8,128)S(1)} %bitcast.12, s32[4,1024]{1,0:T(4,128)S(1)} %copy-done.2, f32[4,192,128]{2,1,0:T(8,128)S(1)} %get-tuple-element.13.before_ref), custom_call_target="tpu_custom_call" | custom-call | flops 10000000 | bytes 1048576 | tf_op jit(solution)/shard_map/pallas_call | solution.py:534
  12.9 0.0 collective-permute-done.in0_ref.y0_ref
  12.9 2.5 %collective-permute-done.1.in1_ref.y1_ref = f32[104,128]{1,0:T(8,128)S(1)} collective-permute-done((f32[104,128]{1,0:T(8,128)S(1)}, f32[104,128]{1,0:T(8,128)S(1)}, u32[]{:S(2)}, u32[]{:S(2)}) %collective-permute-start.1) | collective-permute-done | bytes 53280 | tf_op jit(solution)/shard_map/ppermute | solution.py:504
  15.5 0.1 shard_map.96
  15.6 0.1 collective-permute-start.2
  15.7 6.5 %collective-permute-start.3 = (f32[168,128]{1,0:T(8,128)S(1)}, f32[168,128]{1,0:T(8,128)S(1)}, u32[]{:S(2)}, u32[]{:S(2)}) collective-permute-start(f32[168,128]{1,0:T(8,128)S(1)} %get-tuple-element.19), channel_id=1, source_target_pairs={{0,120},{8,16},{16,8},{24,32},{32,24},{40,48},{48,40},{56,64},{64,... | collective-permute-start | bytes 258056 | tf_op jit(solution)/shard_map/ppermute | solution.py:504
  22.1 0.0 collective-permute-done.2.x0_ref
  22.1 2.2 %collective-permute-done.3.x1_ref = f32[168,128]{1,0:T(8,128)S(1)} collective-permute-done((f32[168,128]{1,0:T(8,128)S(1)}, f32[168,128]{1,0:T(8,128)S(1)}, u32[]{:S(2)}, u32[]{:S(2)}) %collective-permute-start.3) | collective-permute-done | bytes 86048 | tf_op jit(solution)/shard_map/ppermute | solution.py:504
  24.3 2.9 %shard_map.97 = (f32[16,16,8,128]{3,2,1,0:T(8,128)}, f32[16,4,256]{2,1,0:T(4,128)}, f32[16,4,64]{2,1,0:T(4,128)}) custom-call(f32[16,16,8,128]{3,2,1,0:T(8,128)S(1)} %bitcast.13, s32[4,1024]{1,0:T(4,128)S(1)} %copy-done.2, f32[2,160,128]{2,1,0:T(8,128)S(1)} %get-tuple-element.17.joined_ref, f32[104,128]{1,0:T(8,128)S(1)} %collective-permute-done.in0_ref.y0_ref, ...), custom_call_target="tpu_custom_call" | custom-call | flops 10000000 | bytes 1048576 | tf_op jit(solution)/shard_map/pallas_call | solution.py:546
  (4 shorter events, 0.0 us)
Async XLA Ops:
  0.6 0.7 %copy-start.6 = (s32[4,64]{1,0:T(4,128)S(1)}, s32[4,64]{1,0:T(4,128)}, u32[]{:S(2)}) copy-start(s32[4,64]{1,0:T(4,128)} %corner_cell_ref.1) | copy-start | bytes 3076
  0.6 0.7 %copy-start.7 = (s32[8,1]{0,1:T(1,128)S(1)}, s32[8,1]{0,1:T(1,128)}, u32[]{:S(2)}) copy-start(s32[8,1]{0,1:T(1,128)} %param.13) | copy-start | bytes 100
  1.3 1.2 %copy-start = (f32[16,4,4096]{2,1,0:T(4,128)S(1)}, f32[16,4,4096]{2,1,0:T(4,128)}, u32[]{:S(2)}) copy-start(f32[16,4,4096]{2,1,0:T(4,128)} %param.7) | copy-start | bytes 3145732
  2.5 0.7 %copy-start.2 = (s32[4,1024]{1,0:T(4,128)S(1)}, s32[4,1024]{1,0:T(4,128)}, u32[]{:S(2)}) copy-start(s32[4,1024]{1,0:T(4,128)} %cells_ref.5) | copy-start | bytes 49156
  3.3 0.8 %copy-start.3 = (f32[16,4,256]{2,1,0:T(4,128)S(1)}, f32[16,4,256]{2,1,0:T(4,128)}, u32[]{:S(2)}) copy-start(f32[16,4,256]{2,1,0:T(4,128)} %outbox_ref.1) | copy-start | bytes 196612
  4.1 0.8 %copy-start.4 = (f32[16,4,64]{2,1,0:T(4,128)S(1)}, f32[16,4,64]{2,1,0:T(4,128)}, u32[]{:S(2)}) copy-start(f32[16,4,64]{2,1,0:T(4,128)} %corner_ref.1) | copy-start | bytes 49156
  4.9 0.7 %copy-start.5 = (s32[4,256]{1,0:T(4,128)S(1)}, s32[4,256]{1,0:T(4,128)}, u32[]{:S(2)}) copy-start(s32[4,256]{1,0:T(4,128)} %face_cell_ref.1) | copy-start | bytes 12292
  5.5 6.3 %copy-start.1 = (f32[16,4,4096]{2,1,0:T(4,128)S(1)}, f32[16,4,4096]{2,1,0:T(4,128)}, u32[]{:S(2)}) copy-start(f32[16,4,4096]{2,1,0:T(4,128)} %param.7) | copy-start | bytes 3145732
  7.5 5.4 %collective-permute-start = (f32[104,128]{1,0:T(8,128)S(1)}, f32[104,128]{1,0:T(8,128)S(1)}, u32[]{:S(2)}, u32[]{:S(2)}) collective-permute-start(f32[104,128]{1,0:T(8,128)S(1)} %get-tuple-element.14), channel_id=1, source_target_pairs={{0,1},{1,0},{2,3},{3,2},{4,5},{5,4},{6,7},{7,6},{8,9},{9,8},{10,11... | collective-permute-start | bytes 159752 | tf_op jit(solution)/shard_map/ppermute | solution.py:504
  9.2 6.2 %collective-permute-start.1 = (f32[104,128]{1,0:T(8,128)S(1)}, f32[104,128]{1,0:T(8,128)S(1)}, u32[]{:S(2)}, u32[]{:S(2)}) collective-permute-start(f32[104,128]{1,0:T(8,128)S(1)} %get-tuple-element.15), channel_id=1, source_target_pairs={{0,7},{1,2},{2,1},{3,4},{4,3},{5,6},{6,5},{7,0},{8,15},{9,10},{10,... | collective-permute-start | bytes 159752 | tf_op jit(solution)/shard_map/ppermute | solution.py:504
  15.6 6.6 %collective-permute-start.2 = (f32[168,128]{1,0:T(8,128)S(1)}, f32[168,128]{1,0:T(8,128)S(1)}, u32[]{:S(2)}, u32[]{:S(2)}) collective-permute-start(f32[168,128]{1,0:T(8,128)S(1)} %get-tuple-element.18), channel_id=1, source_target_pairs={{0,8},{8,0},{16,24},{24,16},{32,40},{40,32},{48,56},{56,48},{64,72... | collective-permute-start | bytes 258056 | tf_op jit(solution)/shard_map/ppermute | solution.py:504
  15.7 8.6 %collective-permute-start.3 = (f32[168,128]{1,0:T(8,128)S(1)}, f32[168,128]{1,0:T(8,128)S(1)}, u32[]{:S(2)}, u32[]{:S(2)}) collective-permute-start(f32[168,128]{1,0:T(8,128)S(1)} %get-tuple-element.19), channel_id=1, source_target_pairs={{0,120},{8,16},{16,8},{24,32},{32,24},{40,48},{48,40},{56,64},{64,... | collective-permute-start | bytes 258056 | tf_op jit(solution)/shard_map/ppermute | solution.py:504
where the time goes:
time: 27.5 us; the launch traced here: 27.1 us
  starting transfers between devices  10.9 us (40%)
  Pallas kernels  5.93 us (22%)
  local copies, waits for them, and re-layouts  4.9 us (18%)
  waiting for transfers between devices  4.7 us (17%)
  between operations  0.68 us (2%)
    ppermute x4, starting transfers between devices, swapped(): lax.ppermute(value, axis, [(i, partner(i, phase, count)) for i in range(c...  10.9 us
    unnamed x16, local copies, waits for them, and re-layouts  4.9 us
    ppermute x4, waiting for transfers between devices, swapped(): lax.ppermute(value, axis, [(i, partner(i, phase, count)) for i in range(c...  4.7 us
    pallas_call x1, Pallas kernels, body(): call(last_kernel, [VMEM] * 7, [(16, CY, 8, 128), (16, 4, MIG), (16, 4, CO...  2.85 us
    pallas_call x1, Pallas kernels, body(): call(edge_kernel, [SMEM] + [VMEM] * 6, [(Y_ROWS, 128), (Y_ROWS, 128), (2,...  1.93 us
    pallas_call x1, Pallas kernels, body(): call(inner_kernel, [VMEM] * 3, [(2, YY * 8, 128)], [(4, YP * 8, 128), (CY...  1.04 us
  transfers between devices with their start and end apart: 4, of which 2 were waited for; matrix products, arithmetic and copies ran while one was open for 0% of the time, Pallas kernels for 4%

commit v1 on v0

--- a/solution.py
+++ b/solution.py
@@ -41,8 +41,9 @@
     return mass, carried, affine
 
 
-def placed(rows, width, cell, weights, wrap=None):
-    row = lax.broadcasted_iota(jnp.int32, (rows, width), 0)
+def placed(rows, width, cell, weights, wrap=None, row=None):
+    if row is None:
+        row = lax.broadcasted_iota(jnp.int32, (rows, width), 0)
     step = row - cell
     if wrap is not None:
         step = jnp.where(step > wrap // 2, step - wrap, jnp.where(step < -wrap // 2, step + wrap, step))
@@ -106,11 +107,11 @@
     return (slot < counts).astype(F32)
 
 
-def deposit_residents(res_ref, count_ref, terms_ref, total_ref, first, last):
+def deposit_residents(res_ref, count_ref, terms_ref, total_ref, first, last, skip=0):
     row = lax.broadcasted_iota(jnp.int32, (8, 128), 0)
     keep = row < CX
     for y in range(first, last):
-        state = [res_ref[c, y] for c in range(16)]
+        state = [res_ref[c, y - skip] for c in range(16)]
         mass, carried, affine = deposit_terms(state, resident_living(count_ref, y))
         stored = [mass] + carried + affine
         for axis in range(3):
@@ -164,9 +165,80 @@
         finish_node(last)
 
 
-def edge_kernel(count_ref, res_ref, cells_ref, outbox_ref, corner_ref, face_cell_ref, corner_cell_ref,
-                msg0_ref, msg1_ref, ahead_ref, total_ref, terms_ref, stage_ref):
+def decode(cells):
+    number = cells.astype(jnp.int32)
+    living = (number >= 0).astype(F32)
+    return living, number // (CY * NZ), (number // NZ) % CY, number % NZ
+
+
+def deposit_wide(state, cells, total_ref, row_nodes, chunks):
+    rows = len(row_nodes)
+    living, _, cell_y, cell_z = decode(cells)
+    lane = lax.broadcasted_iota(jnp.int32, (2, WIDE), 1)
+    cell_y = cell_y + jnp.where(lane < MIG, 2, jnp.where(lane < MIG + CORNER, 2 + CY, 2 - CY))
+    mass, carried, affine = deposit_terms(state, living)
+    weights = [spline(state[axis]) for axis in range(3)]
+    row = lax.broadcasted_iota(jnp.int32, (rows, WIDE), 0)
+    node = row
+    for k in range(rows):
+        if k == 0:
+            node = row + row_nodes[0]
+        elif row_nodes[k] != row_nodes[k - 1] + 1:
+            node = jnp.where(row >= k, row + (row_nodes[k] - k), node)
+    for g in range(2):
+        depth = placed(NZ, WIDE, row_of(cell_z, g), [row_of(w, g) for w in weights[2]])
+        across, across_moment = placed(
+            rows, WIDE, row_of(cell_y, g), [row_of(w, g) for w in weights[1]], row=node
+        )
+        lines = []
+        zero = jnp.zeros((rows, WIDE), F32)
+        for c in range(4):
+            for e in STEPS:
+                weight = row_of(weights[0][e + 1], g)
+                if c == 0:
+                    plain, moment = (weight * row_of(mass, g)) * across, zero
+                else:
+                    base = row_of(carried[c - 1], g) + e * row_of(affine[3 * (c - 1)], g)
+                    plain = (weight * base) * across + (
+                        weight * row_of(affine[3 * (c - 1) + 1], g)
+                    ) * across_moment
+                    moment = (weight * row_of(affine[3 * (c - 1) + 2], g)) * across
+                lines.append(jnp.concatenate([plain, moment], axis=1))
+        product = scatter_product(jnp.concatenate(lines, axis=0), *depth)
+        for c in range(4):
+            for e in STEPS:
+                row = ((CX if g == 0 else -1) + e) % 8
+                for start, count in chunks:
+                    at = (3 * c + e + 1) * rows + start
+                    total_ref[c, pl.ds(row_nodes[start] * 8 + row, count, stride=8), :] += product[
+                        at : at + count, :
+                    ]
+
+
+def edge_kernel(count_hbm, res_hbm, cells_hbm, outbox_hbm, corner_hbm, face_cell_hbm, corner_cell_hbm,
+                msg0_ref, msg1_ref, ahead_ref, total_ref, wide_ref,
+                terms_ref, stage_ref, res_ref, cells_ref, outbox_ref, corner_ref, face_cell_ref,
+                corner_cell_ref, count_ref, sems):
+    copies = [
+        pltpu.make_async_copy(source, target, sems.at[k])
+        for k, (source, target) in enumerate(
+            [
+                (count_hbm, count_ref),
+                (face_cell_hbm, face_cell_ref),
+                (corner_cell_hbm, corner_cell_ref),
+                (outbox_hbm, outbox_ref),
+                (corner_hbm, corner_ref),
+                (cells_hbm, cells_ref),
+                (res_hbm.at[:, 0:2], res_ref.at[:, 0:2]),
+                (res_hbm.at[:, CY - 2 : CY], res_ref.at[:, 2:4]),
+            ]
+        )
+    ]
+    for copy in copies:
+        copy.start()
     total_ref[...] = jnp.zeros_like(total_ref)
+    for copy in copies[0:5]:
+        copy.wait()
 
     def living_of(width, offset):
         slot = lax.broadcasted_iota(jnp.int32, (4, width), 1)
@@ -202,44 +274,16 @@
                 ahead_ref[side, 33:34, :] = face[side : side + 1, 128:256]
                 ahead_ref[side, 34:40, :] = jnp.zeros((6, 128), F32)
 
-    def decode(cells):
-        number = cells.astype(jnp.int32)
-        living = (number >= 0).astype(F32)
-        return living, number // (CY * NZ), (number // NZ) % CY, number % NZ
-
     def wide(face, corner):
         pairs = jnp.concatenate([join_pairs(corner, 0, 1), join_pairs(corner, 2, 3)], axis=0)
         return jnp.concatenate([face[0:2, :], pairs], axis=1)
 
-    state = [wide(faces[c], corners[c]) for c in range(16)]
-    living, _, cell_y, cell_z = decode(wide(face_cells, corner_cells))
-    lane = lax.broadcasted_iota(jnp.int32, (2, WIDE), 1)
-    cell_y = cell_y + jnp.where(lane < MIG, 2, jnp.where(lane < MIG + CORNER, 2 + CY, 2 - CY))
-    mass, carried, affine = deposit_terms(state, living)
-    weights = [spline(state[axis]) for axis in range(3)]
-    for g in range(2):
-        depth = placed(NZ, WIDE, row_of(cell_z, g), [row_of(w, g) for w in weights[2]])
-        across, across_moment = placed(YP, WIDE, row_of(cell_y, g), [row_of(w, g) for w in weights[1]])
-        lines = []
-        zero = jnp.zeros((YP, WIDE), F32)
-        for c in range(4):
-            for e in STEPS:
-                weight = row_of(weights[0][e + 1], g)
-                if c == 0:
-                    plain, moment = (weight * row_of(mass, g)) * across, zero
-                else:
-                    base = row_of(carried[c - 1], g) + e * row_of(affine[3 * (c - 1)], g)
-                    plain = (weight * base) * across + (
-                        weight * row_of(affine[3 * (c - 1) + 1], g)
-                    ) * across_moment
-                    moment = (weight * row_of(affine[3 * (c - 1) + 2], g)) * across
-                lines.append(jnp.concatenate([plain, moment], axis=1))
-        product = scatter_product(jnp.concatenate(lines, axis=0), *depth)
-        for c in range(4):
-            for e in STEPS:
-                row = ((CX if g == 0 else -1) + e) % 8
-                at = (3 * c + e + 1) * YP
-                total_ref[c, pl.ds(row, YP, stride=8), :] += product[at : at + YP, :]
+    state = [wide(faces[c], corners[c]) for c in range(16)] + [wide(face_cells, corner_cells)]
+    for c, value in enumerate(state):
+        wide_ref[c] = value
+    deposit_wide(
+        state[:16], state[16], total_ref, [0, 1, 2, 17, 18, 19, 100, 101], [(0, 3), (3, 3)]
+    )
 
     state = [face[2:4, :] for face in faces]
     living, cell_x, _, cell_z = decode(face_cells[2:4, :])
@@ -269,8 +313,10 @@
                 line = (3 * c + e + 1) * 8
                 total_ref[c, at : at + 8, :] += product[line : line + 8, :]
 
+    for copy in copies[5:]:
+        copy.wait()
     deposit_residents(res_ref, cells_ref, terms_ref, total_ref, 0, 2)
-    deposit_residents(res_ref, cells_ref, terms_ref, total_ref, CY - 2, CY)
+    deposit_residents(res_ref, cells_ref, terms_ref, total_ref, CY - 2, CY, CY - 4)
 
     for side in range(2):
         for pair in range(2):
@@ -284,8 +330,11 @@
     msg1_ref[...] = stage_ref[1 - parity]
 
 
-def inner_kernel(res_ref, cells_ref, before_ref, grid_ref, total_ref, terms_ref):
+def inner_kernel(res_ref, cells_ref, before_ref, wide_ref, grid_ref, total_ref, terms_ref):
     total_ref[...] = before_ref[...]
+    deposit_wide(
+        [wide_ref[c] for c in range(16)], wide_ref[16], total_ref, list(range(3, 19)), [(0, 14)]
+    )
     deposit_residents(res_ref, cells_ref, terms_ref, total_ref, 2, CY - 2)
     for pair in range(2):
         for yy in range(YY):
@@ -295,7 +344,7 @@
             )
 
 
-def turn_kernel(grid_ref, in0_ref, in1_ref, ahead_ref, joined_ref, msg0_ref, msg1_ref, got_ref, stage_ref):
+def turn_kernel(grid_ref, in1_ref, in0_ref, ahead_ref, joined_ref, msg0_ref, msg1_ref, got_ref, stage_ref):
     parity = lax.axis_index("gy") % 2
     got_ref[parity] = in1_ref[...]
     got_ref[1 - parity] = in0_ref[...]
@@ -370,8 +419,9 @@
     return out + [living * state[15]]
 
 
-def last_kernel(res_ref, cells_ref, joined_ref, y0_ref, y1_ref, x0_ref, x1_ref,
-                out_ref, face_out_ref, corner_out_ref, got_y_ref, got_x_ref, grid_ref, vel_ref, near_ref):
+def last_kernel(res_ref, cells_ref, joined_ref, y1_ref, y0_ref, x1_ref, x0_ref,
+                out_hbm, face_out_hbm, corner_out_hbm, got_y_ref, got_x_ref, grid_ref, vel_ref, near_ref,
+                out_ref, face_out_ref, corner_out_ref, sems):
     parity = lax.axis_index("gy") % 2
     got_y_ref[parity] = y1_ref[...]
     got_y_ref[1 - parity] = y0_ref[...]
@@ -419,49 +469,7 @@
                 near_ref[ex + 1, 0, i, yy - 1] = pltpu.roll(near, 1, 1)
                 near_ref[ex + 1, 2, i, yy - 1] = pltpu.roll(near, 127, 1)
 
-    for side in range(2):
-        def wide_row(k):
-            return jnp.concatenate([got_x_ref[side, a : a + 1, :] for a in k], axis=1)
-
-        base = X_STATES
-        state = [wide_row((base + c, base + 16 + c, base + 32 + c)) for c in range(16)]
-        number = wide_row((base + 48, base + 49, base + 50)).astype(jnp.int32)
-        living = (number >= 0).astype(F32)
-        weights = [spline(state[axis]) for axis in range(3)]
-        depth = placed(NZ, WIDE, number % NZ, weights[2])
-        across, across_moment = placed(YP, WIDE, (number // NZ) % CY + 2, weights[1])
-        lines = []
-        for i in range(3):
-            for e in STEPS:
-                at = ((0 if side == 0 else CX - 1) + e) % 8
-                lines.append(vel_ref[i, pl.ds(at, YP, stride=8), :])
-        product = gather_product(jnp.concatenate(lines, axis=0), *depth)
-        velocity, slopes = contract(product, YP, WIDE, weights[0], across, across_moment, 0, 1)
-        for c, value in enumerate(finished(state, living, velocity, slopes)):
-            face_out_ref[c, side : side + 1, :] = value[:, 0:MIG]
-            corner_out_ref[c, 2 * side : 2 * side + 1, :] = value[:, MIG : MIG + CORNER]
-            corner_out_ref[c, 2 * side + 1 : 2 * side + 2, :] = value[:, MIG + CORNER : WIDE]
-
-    for side in range(2):
-        def face_row(k):
-            return jnp.concatenate([got_y_ref[side, a : a + 1, :] for a in k], axis=1)
-
-        state = [face_row((48 + c, 64 + c)) for c in range(16)]
-        number = face_row((96, 97)).astype(jnp.int32)
-        living = (number >= 0).astype(F32)
-        weights = [spline(state[axis]) for axis in range(3)]
-        depth = placed(NZ, MIG, number % NZ, weights[2])
-        across, across_moment = placed(8, MIG, jnp.maximum(number, 0) // (CY * NZ), weights[0], 8)
-        lines = []
-        for i in range(3):
-            for e in STEPS:
-                at = ((0 if side == 0 else CY - 1) + 2 + e) * 8
-                lines.append(vel_ref[i, at : at + 8, :])
-        product = gather_product(jnp.concatenate(lines, axis=0), *depth)
-        velocity, slopes = contract(product, 8, MIG, weights[1], across, across_moment, 1, 0)
-        for c, value in enumerate(finished(state, living, velocity, slopes)):
-            face_out_ref[c, 2 + side : 3 + side, :] = value
-
+    copies = []
     for y in range(CY):
         state = [res_ref[c, y] for c in range(16)]
         living = resident_living(cells_ref, y)
@@ -493,6 +501,63 @@
             slopes.append(slope)
         for c, value in enumerate(finished(state, living, velocity, slopes)):
             out_ref[c, y] = value
+        if y % 4 == 3:
+            copies.append(
+                pltpu.make_async_copy(
+                    out_ref.at[:, y - 3 : y + 1], out_hbm.at[:, y - 3 : y + 1], sems.at[y // 4]
+                )
+            )
+            copies[-1].start()
+
+    for side in range(2):
+        def wide_row(k):
+            return jnp.concatenate([got_x_ref[side, a : a + 1, :] for a in k], axis=1)
+
+        base = X_STATES
+        state = [wide_row((base + c, base + 16 + c, base + 32 + c)) for c in range(16)]
+        number = wide_row((base + 48, base + 49, base + 50)).astype(jnp.int32)
+        living = (number >= 0).astype(F32)
+        weights = [spline(state[axis]) for axis in range(3)]
+        depth = placed(NZ, WIDE, number % NZ, weights[2])
+        across, across_moment = placed(YP, WIDE, (number // NZ) % CY + 2, weights[1])
+        lines = []
+        for i in range(3):
+            for e in STEPS:
+                at = ((0 if side == 0 else CX - 1) + e) % 8
+                lines.append(vel_ref[i, pl.ds(at, YP, stride=8), :])
+        product = gather_product(jnp.concatenate(lines, axis=0), *depth)
+        velocity, slopes = contract(product, YP, WIDE, weights[0], across, across_moment, 0, 1)
+        for c, value in enumerate(finished(state, living, velocity, slopes)):
+            face_out_ref[c, side : side + 1, :] = value[:, 0:MIG]
+            corner_out_ref[c, 2 * side : 2 * side + 1, :] = value[:, MIG : MIG + CORNER]
+            corner_out_ref[c, 2 * side + 1 : 2 * side + 2, :] = value[:, MIG + CORNER : WIDE]
+
+    for side in range(2):
+        def face_row(k):
+            return jnp.concatenate([got_y_ref[side, a : a + 1, :] for a in k], axis=1)
+
+        state = [face_row((48 + c, 64 + c)) for c in range(16)]
+        number = face_row((96, 97)).astype(jnp.int32)
+        living = (number >= 0).astype(F32)
+        weights = [spline(state[axis]) for axis in range(3)]
+        depth = placed(NZ, MIG, number % NZ, weights[2])
+        across, across_moment = placed(8, MIG, jnp.maximum(number, 0) // (CY * NZ), weights[0], 8)
+        lines = []
+        for i in range(3):
+            for e in STEPS:
+                at = ((0 if side == 0 else CY - 1) + 2 + e) * 8
+                lines.append(vel_ref[i, at : at + 8, :])
+        product = gather_product(jnp.concatenate(lines, axis=0), *depth)
+        velocity, slopes = contract(product, 8, MIG, weights[1], across, across_moment, 1, 0)
+        for c, value in enumerate(finished(state, living, velocity, slopes)):
+            face_out_ref[c, 2 + side : 3 + side, :] = value
+
+    copies.append(pltpu.make_async_copy(face_out_ref, face_out_hbm, sems.at[4]))
+    copies.append(pltpu.make_async_copy(corner_out_ref, corner_out_hbm, sems.at[5]))
+    for copy in copies[-2:]:
+        copy.start()
+    for copy in copies:
+        copy.wait()
 
 
 def partner(index, phase, count):
@@ -505,57 +570,85 @@
 
 
 VMEM = pl.BlockSpec(memory_space=pltpu.VMEM)
-SMEM = pl.BlockSpec(memory_space=pltpu.SMEM)
-
-
-def call(kernel, in_specs, out_shapes, scratch, flops):
+HBM = pl.BlockSpec(memory_space=pltpu.HBM)
+
+
+def scratch(shape, dtype=F32):
+    return pltpu.VMEM(shape, dtype)
+
+
+def call(kernel, in_specs, out_spec, out_shapes, scratch_shapes, flops, limit=24):
     return pl.pallas_call(
         kernel,
         in_specs=in_specs,
-        out_specs=[VMEM] * len(out_shapes),
+        out_specs=[out_spec] * len(out_shapes),
         out_shape=[jax.ShapeDtypeStruct(shape, F32) for shape in out_shapes],
-        scratch_shapes=[pltpu.VMEM(shape, F32) for shape in scratch],
-        compiler_params=pltpu.CompilerParams(vmem_limit_bytes=24 * 1024 * 1024),
+        scratch_shapes=scratch_shapes,
+        compiler_params=pltpu.CompilerParams(vmem_limit_bytes=limit * 1024 * 1024),
         cost_estimate=pl.CostEstimate(flops=flops, bytes_accessed=1 << 20, transcendentals=0),
     )
 
 
 def body(residents, cell_count, outbox, corner_box, face_cell, corner_cell, mig_count):
     res = residents.reshape(16, CX, CY, 2, 128).transpose(0, 2, 3, 1, 4).reshape(16, CY, 8, 128)
-    msg0, msg1, ahead, total = call(
+    msg0, msg1, ahead, total, wide = call(
         edge_kernel,
-        [SMEM] + [VMEM] * 6,
-        [(Y_ROWS, 128), (Y_ROWS, 128), (2, 40, 128), (4, YP * 8, 128)],
-        [(CY, 22, 8, 128), (2, Y_ROWS, 128)],
+        [HBM] * 7,
+        VMEM,
+        [(Y_ROWS, 128), (Y_ROWS, 128), (2, 40, 128), (4, YP * 8, 128), (17, 2, WIDE)],
+        [
+            scratch((CY, 22, 8, 128)),
+            scratch((2, Y_ROWS, 128)),
+            scratch((16, 4, 8, 128)),
+            scratch((CX, CY * NZ), jnp.int32),
+            scratch((16, 4, MIG)),
+            scratch((16, 4, CORNER)),
+            scratch((4, MIG), jnp.int32),
+            scratch((4, CORNER), jnp.int32),
+            pltpu.SMEM((8,), jnp.int32),
+            pltpu.SemaphoreType.DMA((8,)),
+        ],
         10_000_000,
+        62,
     )(mig_count.reshape(8), res, cell_count, outbox, corner_box, face_cell, corner_cell)
+    y0 = swapped(msg0, "gy", 0)
     y1 = swapped(msg1, "gy", 1)
-    y0 = swapped(msg0, "gy", 0)
     (grid,) = call(
-        inner_kernel, [VMEM] * 3, [(2, YY * 8, 128)], [(4, YP * 8, 128), (CY, 22, 8, 128)], 10_000_000
-    )(res, cell_count, total)
+        inner_kernel,
+        [VMEM] * 4,
+        VMEM,
+        [(2, YY * 8, 128)],
+        [scratch((4, YP * 8, 128)), scratch((CY, 22, 8, 128))],
+        10_000_000,
+    )(res, cell_count, total, wide)
     joined, msg0, msg1 = call(
         turn_kernel,
         [VMEM] * 4,
+        VMEM,
         [(2, YY * 8, 128), (X_ROWS, 128), (X_ROWS, 128)],
-        [(2, Y_ROWS, 128), (2, X_ROWS, 128)],
+        [scratch((2, Y_ROWS, 128)), scratch((2, X_ROWS, 128))],
         1_000_000,
-    )(grid, y0, y1, ahead)
+    )(grid, y1, y0, ahead)
+    x0 = swapped(msg0, "gx", 0)
     x1 = swapped(msg1, "gx", 1)
-    x0 = swapped(msg0, "gx", 0)
     out, face_out, corner_out = call(
         last_kernel,
         [VMEM] * 7,
+        HBM,
         [(16, CY, 8, 128), (16, 4, MIG), (16, 4, CORNER)],
         [
-            (2, Y_ROWS, 128),
-            (2, X_ROWS, 128),
-            (2, YY * 8, 128),
-            (3, YP * 8, 128),
-            (3, 3, 3, CY + 2, 8, 128),
+            scratch((2, Y_ROWS, 128)),
+            scratch((2, X_ROWS, 128)),
+            scratch((2, YY * 8, 128)),
+            scratch((3, YP * 8, 128)),
+            scratch((3, 3, 3, CY + 2, 8, 128)),
+            scratch((16, CY, 8, 128)),
+            scratch((16, 4, MIG)),
+            scratch((16, 4, CORNER)),
+            pltpu.SemaphoreType.DMA((6,)),
         ],
         10_000_000,
-    )(res, cell_count, joined, y0, y1, x0, x1)
+    )(res, cell_count, joined, y1, y0, x1, x0)
     out = out.reshape(16, CY, 2, CX, 128).transpose(0, 3, 1, 2, 4).reshape(16, CX, CY * 256)
     return out, face_out, corner_out
 

time: 27.5 us -> 22.6 us (0.82)
  local copies, waits for them, and re-layouts: 4.9 us -> 1.81 us
  starting transfers between devices: 10.9 us -> 8.97 us
  Pallas kernels: 5.93 us -> 7.32 us
  waiting for transfers between devices: 4.7 us -> 3.62 us
    unnamed x16 -> x10, local copies, waits for them, and re-layouts: 4.9 us -> 1.81 us
    ppermute x4, starting transfers between devices: 10.9 us -> 8.97 us  [swapped(): lax.ppermute(value, axis, [(i, partner(i, phase, count)) for i in range(c...]
    pallas_call x4, Pallas kernels: 5.93 us -> 7.32 us  [the longest x1 3 us: body(): call(edge_kernel, [HBM] * 7, VMEM, [(Y_ROWS, 128), (Y_ROWS, 128), (2, 40,...]
    ppermute x4, waiting for transfers between devices: 4.7 us -> 3.62 us  [swapped(): lax.ppermute(value, axis, [(i, partner(i, phase, count)) for i in range(c...]
  transfers between devices with their start and end apart: 4 -> 4, of which waited for: 2 -> 2; matrix products, arithmetic and copies ran while one was open for 0% -> 0% of each run, Pallas kernels for 4% -> 7%
where the time goes in v1:
time: 22.6 us; the launch traced here: 22.4 us
  starting transfers between devices  8.97 us (40%)
  Pallas kernels  7.32 us (32%)
  waiting for transfers between devices  3.62 us (16%)
  local copies, waits for them, and re-layouts  1.81 us (8%)
  between operations  0.69 us (3%)
    ppermute x4, starting transfers between devices, swapped(): lax.ppermute(value, axis, [(i, partner(i, phase, count)) for i in range(c...  8.97 us
    ppermute x4, waiting for transfers between devices, swapped(): lax.ppermute(value, axis, [(i, partner(i, phase, count)) for i in range(c...  3.62 us
    pallas_call x1, Pallas kernels, body(): call(edge_kernel, [HBM] * 7, VMEM, [(Y_ROWS, 128), (Y_ROWS, 128), (2, 40,...  3 us
    pallas_call x1, Pallas kernels, body(): call(last_kernel, [VMEM] * 7, HBM, [(16, CY, 8, 128), (16, 4, MIG), (16,...  2.75 us
    unnamed x10, local copies, waits for them, and re-layouts  1.81 us
    pallas_call x1, Pallas kernels, body(): call(inner_kernel, [VMEM] * 4, VMEM, [(2, YY * 8, 128)], [scratch((4, YP...  1.46 us
  transfers between devices with their start and end apart: 4, of which 2 were waited for; matrix products, arithmetic and copies ran while one was open for 0% of the time, Pallas kernels for 7%

profile of v1, /device:TPU:0, one launch (start us, length us, event | category | flops | bytes accessed | tf_op | source)
XLA Modules:
  0.0 22.4 jit_solution(5475055853699185978)
XLA Ops:
  0.6 0.0 copy-start
  0.6 0.0 copy-start.2
  0.7 3.0 %shard_map.94 = (f32[104,128]{1,0:T(8,128)}, f32[104,128]{1,0:T(8,128)}, f32[2,40,128]{2,1,0:T(8,128)}, f32[4,192,128]{2,1,0:T(8,128)}, f32[17,2,384]{2,1,0:T(2,128)}) custom-call(s32[8]{0:T(128)} %bitcast.14, f32[16,16,8,128]{3,2,1,0:T(8,128)} %bitcast.11, s32[4,1024]{1,0:T(4,128)} %cells_ref.3, f32[16,4,256]{2,1,0:T(4,128)} %outbox_hbm.1, ...), custom_call_target="tpu_custom_call" | custom-call | flops 10000000 | bytes 1048576 | tf_op jit(solution)/shard_map/pallas_call | solution.py:594
  3.7 3.9 %collective-permute-start = (f32[104,128]{1,0:T(8,128)}, f32[104,128]{1,0:T(8,128)S(1)}, u32[]{:S(2)}, u32[]{:S(2)}) collective-permute-start(f32[104,128]{1,0:T(8,128)} %get-tuple-element.16), channel_id=1, source_target_pairs={{0,7},{1,2},{2,1},{3,4},{4,3},{5,6},{6,5},{7,0},{8,15},{9,10},{10,... | collective-permute-start | bytes 159752 | tf_op jit(solution)/shard_map/ppermute | solution.py:569
  7.6 0.0 collective-permute-start.1
  7.6 0.0 copy-done
  7.6 0.0 copy-done.2
  7.6 0.0 copy-start.1
  7.6 1.0 %copy-done.1 = f32[4,192,128]{2,1,0:T(8,128)S(1)} copy-done((f32[4,192,128]{2,1,0:T(8,128)S(1)}, f32[4,192,128]{2,1,0:T(8,128)}, u32[]{:S(2)}) %copy-start.1) | copy-done | bytes 393240
  8.6 0.0 copy-start.3
  8.6 0.8 %copy-done.3 = f32[17,2,384]{2,1,0:T(2,128)S(1)} copy-done((f32[17,2,384]{2,1,0:T(2,128)S(1)}, f32[17,2,384]{2,1,0:T(2,128)}, u32[]{:S(2)}) %copy-start.3) | copy-done | bytes 52248
  9.4 0.0 copy-start.4
  9.4 1.5 %shard_map.95.grid_ref = f32[2,160,128]{2,1,0:T(8,128)S(1)} custom-call(f32[16,16,8,128]{3,2,1,0:T(8,128)S(1)} %bitcast.12, s32[4,1024]{1,0:T(4,128)S(1)} %copy-done.2, f32[4,192,128]{2,1,0:T(8,128)S(1)} %copy-done.1, f32[17,2,384]{2,1,0:T(2,128)S(1)} %copy-done.3), custom_call_target="tpu_custom_call" | custom-call | flops 10000000 | bytes 1048576 | tf_op jit(solution)/shard_map/pallas_call | solution.py:616
  10.9 0.0 collective-permute-done.in1_ref.y1_ref
  10.9 1.1 %collective-permute-done.1.in0_ref.y0_ref = f32[104,128]{1,0:T(8,128)S(1)} collective-permute-done((f32[104,128]{1,0:T(8,128)}, f32[104,128]{1,0:T(8,128)S(1)}, u32[]{:S(2)}, u32[]{:S(2)}) %collective-permute-start.1) | collective-permute-done | bytes 53280 | tf_op jit(solution)/shard_map/ppermute | solution.py:569
  11.9 0.0 copy-done.4
  11.9 0.1 shard_map.96
  12.1 5.0 %collective-permute-start.2 = (f32[168,128]{1,0:T(8,128)S(1)}, f32[168,128]{1,0:T(8,128)S(1)}, u32[]{:S(2)}, u32[]{:S(2)}) collective-permute-start(f32[168,128]{1,0:T(8,128)S(1)} %get-tuple-element.20), channel_id=1, source_target_pairs={{0,120},{8,16},{16,8},{24,32},{32,24},{40,48},{48,40},{56,64},{64,... | collective-permute-start | bytes 258056 | tf_op jit(solution)/shard_map/ppermute | solution.py:569
  17.1 0.0 collective-permute-start.3
  17.1 2.6 %collective-permute-done.2.x1_ref = f32[168,128]{1,0:T(8,128)S(1)} collective-permute-done((f32[168,128]{1,0:T(8,128)S(1)}, f32[168,128]{1,0:T(8,128)S(1)}, u32[]{:S(2)}, u32[]{:S(2)}) %collective-permute-start.2) | collective-permute-done | bytes 86048 | tf_op jit(solution)/shard_map/ppermute | solution.py:569
  19.7 0.0 collective-permute-done.3.x0_ref
  19.7 2.8 %shard_map.97 = (f32[16,16,8,128]{3,2,1,0:T(8,128)}, f32[16,4,256]{2,1,0:T(4,128)}, f32[16,4,64]{2,1,0:T(4,128)}) custom-call(f32[16,16,8,128]{3,2,1,0:T(8,128)S(1)} %bitcast.13, s32[4,1024]{1,0:T(4,128)S(1)} %copy-done.2, f32[2,160,128]{2,1,0:T(8,128)S(1)} %get-tuple-element.19.joined_ref, f32[104,128]{1,0:T(8,128)S(1)} %collective-permute-done.in1_ref.y1_ref, ...), custom_call_target="tpu_custom_call" | custom-call | flops 10000000 | bytes 1048576 | tf_op jit(solution)/shard_map/pallas_call | solution.py:634
Async XLA Ops:
  0.6 7.0 %copy-start = (f32[16,4,4096]{2,1,0:T(4,128)S(1)}, f32[16,4,4096]{2,1,0:T(4,128)}, u32[]{:S(2)}) copy-start(f32[16,4,4096]{2,1,0:T(4,128)} %param.7) | copy-start | bytes 3145732
  0.6 7.0 %copy-start.2 = (s32[4,1024]{1,0:T(4,128)S(1)}, s32[4,1024]{1,0:T(4,128)}, u32[]{:S(2)}) copy-start(s32[4,1024]{1,0:T(4,128)} %cells_ref.3) | copy-start | bytes 49156
  3.7 7.2 %collective-permute-start = (f32[104,128]{1,0:T(8,128)}, f32[104,128]{1,0:T(8,128)S(1)}, u32[]{:S(2)}, u32[]{:S(2)}) collective-permute-start(f32[104,128]{1,0:T(8,128)} %get-tuple-element.16), channel_id=1, source_target_pairs={{0,7},{1,2},{2,1},{3,4},{4,3},{5,6},{6,5},{7,0},{8,15},{9,10},{10,... | collective-permute-start | bytes 159752 | tf_op jit(solution)/shard_map/ppermute | solution.py:569
  7.6 4.3 %collective-permute-start.1 = (f32[104,128]{1,0:T(8,128)}, f32[104,128]{1,0:T(8,128)S(1)}, u32[]{:S(2)}, u32[]{:S(2)}) collective-permute-start(f32[104,128]{1,0:T(8,128)} %get-tuple-element.17), channel_id=1, source_target_pairs={{0,1},{1,0},{2,3},{3,2},{4,5},{5,4},{6,7},{7,6},{8,9},{9,8},{10,11... | collective-permute-start | bytes 159752 | tf_op jit(solution)/shard_map/ppermute | solution.py:569
  7.6 1.0 %copy-start.1 = (f32[4,192,128]{2,1,0:T(8,128)S(1)}, f32[4,192,128]{2,1,0:T(8,128)}, u32[]{:S(2)}) copy-start(f32[4,192,128]{2,1,0:T(8,128)} %get-tuple-element.14.before_ref) | copy-start | bytes 1179652
  8.6 0.8 %copy-start.3 = (f32[17,2,384]{2,1,0:T(2,128)S(1)}, f32[17,2,384]{2,1,0:T(2,128)}, u32[]{:S(2)}) copy-start(f32[17,2,384]{2,1,0:T(2,128)} %get-tuple-element.15.wide_ref) | copy-start | bytes 156676
  9.4 2.5 %copy-start.4 = (f32[2,40,128]{2,1,0:T(8,128)S(1)}, f32[2,40,128]{2,1,0:T(8,128)}, u32[]{:S(2)}) copy-start(f32[2,40,128]{2,1,0:T(8,128)} %get-tuple-element.18.ahead_ref) | copy-start | bytes 122884
  12.1 7.6 %collective-permute-start.2 = (f32[168,128]{1,0:T(8,128)S(1)}, f32[168,128]{1,0:T(8,128)S(1)}, u32[]{:S(2)}, u32[]{:S(2)}) collective-permute-start(f32[168,128]{1,0:T(8,128)S(1)} %get-tuple-element.20), channel_id=1, source_target_pairs={{0,120},{8,16},{16,8},{24,32},{32,24},{40,48},{48,40},{56,64},{64,... | collective-permute-start | bytes 258056 | tf_op jit(solution)/shard_map/ppermute | solution.py:569
  17.1 2.6 %collective-permute-start.3 = (f32[168,128]{1,0:T(8,128)S(1)}, f32[168,128]{1,0:T(8,128)S(1)}, u32[]{:S(2)}, u32[]{:S(2)}) collective-permute-start(f32[168,128]{1,0:T(8,128)S(1)} %get-tuple-element.21), channel_id=1, source_target_pairs={{0,8},{8,0},{16,24},{24,16},{32,40},{40,32},{48,56},{56,48},{64,72... | collective-permute-start | bytes 258056 | tf_op jit(solution)/shard_map/ppermute | solution.py:569

commit v2 on v1

--- a/solution.py
+++ b/solution.py
@@ -72,11 +72,11 @@
 def scatter_product(lhs, depth_plain, depth_moment):
     rhs = jnp.concatenate([depth_plain, depth_moment], axis=1)
     rhs = jnp.concatenate(split(rhs), axis=0)
-    coarse, fine = split(lhs)
-    dims = (((1,), (1,)), ((), ()))
-    return lax.dot_general(coarse, rhs, dims, preferred_element_type=F32) + lax.dot_general(
-        fine, rhs, dims, preferred_element_type=F32
+    rows = lhs.shape[0]
+    product = lax.dot_general(
+        jnp.concatenate(split(lhs), axis=0), rhs, (((1,), (1,)), ((), ())), preferred_element_type=F32
     )
+    return product[0:rows] + product[rows : 2 * rows]
 
 
 def row_of(value, g):
@@ -107,11 +107,11 @@
     return (slot < counts).astype(F32)
 
 
-def deposit_residents(res_ref, count_ref, terms_ref, total_ref, first, last, skip=0):
+def deposit_residents(res_ref, count_ref, terms_ref, total_ref, first, last):
     row = lax.broadcasted_iota(jnp.int32, (8, 128), 0)
     keep = row < CX
     for y in range(first, last):
-        state = [res_ref[c, y - skip] for c in range(16)]
+        state = [res_ref[c, y] for c in range(16)]
         mass, carried, affine = deposit_terms(state, resident_living(count_ref, y))
         stored = [mass] + carried + affine
         for axis in range(3):
@@ -215,38 +215,24 @@
                     ]
 
 
-def edge_kernel(count_hbm, res_hbm, cells_hbm, outbox_hbm, corner_hbm, face_cell_hbm, corner_cell_hbm,
-                msg0_ref, msg1_ref, ahead_ref, total_ref, wide_ref,
-                terms_ref, stage_ref, res_ref, cells_ref, outbox_ref, corner_ref, face_cell_ref,
-                corner_cell_ref, count_ref, sems):
-    copies = [
-        pltpu.make_async_copy(source, target, sems.at[k])
-        for k, (source, target) in enumerate(
-            [
-                (count_hbm, count_ref),
-                (face_cell_hbm, face_cell_ref),
-                (corner_cell_hbm, corner_cell_ref),
-                (outbox_hbm, outbox_ref),
-                (corner_hbm, corner_ref),
-                (cells_hbm, cells_ref),
-                (res_hbm.at[:, 0:2], res_ref.at[:, 0:2]),
-                (res_hbm.at[:, CY - 2 : CY], res_ref.at[:, 2:4]),
-            ]
-        )
-    ]
-    for copy in copies:
-        copy.start()
+def open_kernel(mark_ref):
+    mark_ref[...] = jnp.zeros_like(mark_ref)
+
+
+def edge_kernel(mark_ref, count_ref, res_ref, cells_ref, outbox_ref, corner_ref, face_cell_ref,
+                corner_cell_ref, msg0_ref, msg1_ref, ahead_ref, total_ref, wide_ref, terms_ref, stage_ref):
     total_ref[...] = jnp.zeros_like(total_ref)
-    for copy in copies[0:5]:
-        copy.wait()
+
+    def count(k, width):
+        return jnp.broadcast_to(count_ref[0:1, k : k + 1], (4, width))
 
     def living_of(width, offset):
         slot = lax.broadcasted_iota(jnp.int32, (4, width), 1)
         row = lax.broadcasted_iota(jnp.int32, (4, width), 0)
         counts = jnp.where(
             row < 2,
-            jnp.where(row == 0, count_ref[offset], count_ref[offset + 1]),
-            jnp.where(row == 2, count_ref[offset + 2], count_ref[offset + 3]),
+            jnp.where(row == 0, count(offset, width), count(offset + 1, width)),
+            jnp.where(row == 2, count(offset + 2, width), count(offset + 3, width)),
         )
         return slot < counts
 
@@ -313,10 +299,8 @@
                 line = (3 * c + e + 1) * 8
                 total_ref[c, at : at + 8, :] += product[line : line + 8, :]
 
-    for copy in copies[5:]:
-        copy.wait()
     deposit_residents(res_ref, cells_ref, terms_ref, total_ref, 0, 2)
-    deposit_residents(res_ref, cells_ref, terms_ref, total_ref, CY - 2, CY, CY - 4)
+    deposit_residents(res_ref, cells_ref, terms_ref, total_ref, CY - 2, CY)
 
     for side in range(2):
         for pair in range(2):
@@ -577,40 +561,29 @@
     return pltpu.VMEM(shape, dtype)
 
 
-def call(kernel, in_specs, out_spec, out_shapes, scratch_shapes, flops, limit=24):
+def call(kernel, in_specs, out_spec, out_shapes, scratch_shapes, flops):
     return pl.pallas_call(
         kernel,
         in_specs=in_specs,
         out_specs=[out_spec] * len(out_shapes),
         out_shape=[jax.ShapeDtypeStruct(shape, F32) for shape in out_shapes],
         scratch_shapes=scratch_shapes,
-        compiler_params=pltpu.CompilerParams(vmem_limit_bytes=limit * 1024 * 1024),
+        compiler_params=pltpu.CompilerParams(vmem_limit_bytes=24 * 1024 * 1024),
         cost_estimate=pl.CostEstimate(flops=flops, bytes_accessed=1 << 20, transcendentals=0),
     )
 
 
 def body(residents, cell_count, outbox, corner_box, face_cell, corner_cell, mig_count):
     res = residents.reshape(16, CX, CY, 2, 128).transpose(0, 2, 3, 1, 4).reshape(16, CY, 8, 128)
+    (mark,) = call(open_kernel, [], VMEM, [(8, 128)], [], 10_000_000_000)()
     msg0, msg1, ahead, total, wide = call(
         edge_kernel,
-        [HBM] * 7,
+        [VMEM] * 8,
         VMEM,
         [(Y_ROWS, 128), (Y_ROWS, 128), (2, 40, 128), (4, YP * 8, 128), (17, 2, WIDE)],
-        [
-            scratch((CY, 22, 8, 128)),
-            scratch((2, Y_ROWS, 128)),
-            scratch((16, 4, 8, 128)),
-            scratch((CX, CY * NZ), jnp.int32),
-            scratch((16, 4, MIG)),
-            scratch((16, 4, CORNER)),
-            scratch((4, MIG), jnp.int32),
-            scratch((4, CORNER), jnp.int32),
-            pltpu.SMEM((8,), jnp.int32),
-            pltpu.SemaphoreType.DMA((8,)),
-        ],
+        [scratch((CY, 22, 8, 128)), scratch((2, Y_ROWS, 128))],
         10_000_000,
-        62,
-    )(mig_count.reshape(8), res, cell_count, outbox, corner_box, face_cell, corner_cell)
+    )(mark, mig_count.reshape(1, 8), res, cell_count, outbox, corner_box, face_cell, corner_cell)
     y0 = swapped(msg0, "gy", 0)
     y1 = swapped(msg1, "gy", 1)
     (grid,) = call(

time: 22.6 us -> 21.7 us (0.960)
  Pallas kernels: 7.32 us -> 5.45 us
  waiting for transfers between devices: 3.62 us -> 5.21 us
  local copies, waits for them, and re-layouts: 1.81 us -> 1.24 us
    pallas_call x1 -> x2, Pallas kernels: 3 us -> 1.1 us  [the longest x1 1.09 us: body(): call(edge_kernel, [VMEM] * 8, VMEM, [(Y_ROWS, 128), (Y_ROWS, 128), (2, 40...]
    ppermute x4, waiting for transfers between devices: 3.62 us -> 5.21 us  [swapped(): lax.ppermute(value, axis, [(i, partner(i, phase, count)) for i in range(c...]
    unnamed x10 -> x14, local copies, waits for them, and re-layouts: 1.81 us -> 1.24 us
  transfers between devices with their start and end apart: 4 -> 4, of which waited for: 2 -> 3; matrix products, arithmetic and copies ran while one was open for 0% -> 0% of each run, Pallas kernels for 7% -> 7%
where the time goes in v2:
time: 21.7 us; the launch traced here: 21.6 us
  starting transfers between devices  8.96 us (41%)
  Pallas kernels  5.45 us (25%)
  waiting for transfers between devices  5.21 us (24%)
  local copies, waits for them, and re-layouts  1.24 us (6%)
  between operations  0.71 us (3%)
    ppermute x4, starting transfers between devices, swapped(): lax.ppermute(value, axis, [(i, partner(i, phase, count)) for i in range(c...  8.96 us
    ppermute x4, waiting for transfers between devices, swapped(): lax.ppermute(value, axis, [(i, partner(i, phase, count)) for i in range(c...  5.21 us
    pallas_call x1, Pallas kernels, body(): call(last_kernel, [VMEM] * 7, HBM, [(16, CY, 8, 128), (16, 4, MIG), (16,...  2.76 us
    pallas_call x1, Pallas kernels, body(): call(inner_kernel, [VMEM] * 4, VMEM, [(2, YY * 8, 128)], [scratch((4, YP...  1.48 us
    unnamed x14, local copies, waits for them, and re-layouts  1.24 us
    pallas_call x1, Pallas kernels, body(): call(edge_kernel, [VMEM] * 8, VMEM, [(Y_ROWS, 128), (Y_ROWS, 128), (2, 40...  1.09 us
  transfers between devices with their start and end apart: 4, of which 3 were waited for; matrix products, arithmetic and copies ran while one was open for 0% of the time, Pallas kernels for 7%

profile of v2, /device:TPU:0, one launch (start us, length us, event | category | flops | bytes accessed | tf_op | source)
XLA Modules:
  0.0 21.6 jit_solution(9489112621746115963)
XLA Ops:
  0.6 0.0 copy-start.1
  0.6 0.0 copy-start.3
  0.7 0.0 copy-start.2
  0.7 0.0 copy-start
  0.7 0.0 copy-start.4
  0.7 0.0 copy-start.5
  0.7 0.0 copy-start.6
  0.7 0.6 %copy-done.1 = s32[4,1024]{1,0:T(4,128)S(1)} copy-done((s32[4,1024]{1,0:T(4,128)S(1)}, s32[4,1024]{1,0:T(4,128)}, u32[]{:S(2)}) %copy-start.1) | copy-done | bytes 16408
  1.4 0.1 copy-done.3
  1.4 0.1 copy-done.2
  1.5 0.4 %copy-done = f32[16,4,4096]{2,1,0:T(4,128)S(1)} copy-done((f32[16,4,4096]{2,1,0:T(4,128)S(1)}, f32[16,4,4096]{2,1,0:T(4,128)}, u32[]{:S(2)}) %copy-start) | copy-done | bytes 1048600
  1.9 0.0 copy-done.4
  1.9 1.1 %shard_map.95 = (f32[104,128]{1,0:T(8,128)S(1)}, f32[104,128]{1,0:T(8,128)S(1)}, f32[2,40,128]{2,1,0:T(8,128)S(1)}, f32[4,192,128]{2,1,0:T(8,128)S(1)}, f32[17,2,384]{2,1,0:T(2,128)S(1)}) custom-call(f32[8,128]{1,0:T(8,128)S(1)} %shard_map.94.mark_ref, s32[1,8]{1,0:T(1,128)S(1)} %bitcast.14, f32[16,16,8,128]{3,2,1,0:T(8,128)S(1)} %bitcast.11, ...), custom_call_target="tpu_custom_call" | custom-call | flops 10000000 | bytes 1048576 | tf_op jit(solution)/shard_map/pallas_call | solution.py:579
  3.0 3.9 %collective-permute-start = (f32[104,128]{1,0:T(8,128)S(1)}, f32[104,128]{1,0:T(8,128)S(1)}, u32[]{:S(2)}, u32[]{:S(2)}) collective-permute-start(f32[104,128]{1,0:T(8,128)S(1)} %get-tuple-element.16), channel_id=1, source_target_pairs={{0,7},{1,2},{2,1},{3,4},{4,3},{5,6},{6,5},{7,0},{8,15},{9,10},{10,... | collective-permute-start | bytes 159752 | tf_op jit(solution)/shard_map/ppermute | solution.py:553
  7.0 0.0 collective-permute-start.1
  7.0 1.5 %shard_map.96.grid_ref = f32[2,160,128]{2,1,0:T(8,128)S(1)} custom-call(f32[16,16,8,128]{3,2,1,0:T(8,128)S(1)} %bitcast.12, s32[4,1024]{1,0:T(4,128)S(1)} %copy-done.1, f32[4,192,128]{2,1,0:T(8,128)S(1)} %get-tuple-element.14.before_ref, f32[17,2,384]{2,1,0:T(2,128)S(1)} %get-tuple-element.15.wide_ref), custom_call_target="tpu_custom_call" | custom-call | flops 10000000 | bytes 1048576 | tf_op jit(solution)/shard_map/pallas_call | solution.py:589
  8.5 0.9 %collective-permute-done.in1_ref.y1_ref = f32[104,128]{1,0:T(8,128)S(1)} collective-permute-done((f32[104,128]{1,0:T(8,128)S(1)}, f32[104,128]{1,0:T(8,128)S(1)}, u32[]{:S(2)}, u32[]{:S(2)}) %collective-permute-start) | collective-permute-done | bytes 53280 | tf_op jit(solution)/shard_map/ppermute | solution.py:553
  9.4 1.7 %collective-permute-done.1.in0_ref.y0_ref = f32[104,128]{1,0:T(8,128)S(1)} collective-permute-done((f32[104,128]{1,0:T(8,128)S(1)}, f32[104,128]{1,0:T(8,128)S(1)}, u32[]{:S(2)}, u32[]{:S(2)}) %collective-permute-start.1) | collective-permute-done | bytes 53280 | tf_op jit(solution)/shard_map/ppermute | solution.py:553
  11.1 0.1 shard_map.97
  11.2 5.0 %collective-permute-start.2 = (f32[168,128]{1,0:T(8,128)S(1)}, f32[168,128]{1,0:T(8,128)S(1)}, u32[]{:S(2)}, u32[]{:S(2)}) collective-permute-start(f32[168,128]{1,0:T(8,128)S(1)} %get-tuple-element.20), channel_id=1, source_target_pairs={{0,120},{8,16},{16,8},{24,32},{32,24},{40,48},{48,40},{56,64},{64,... | collective-permute-start | bytes 258056 | tf_op jit(solution)/shard_map/ppermute | solution.py:553
  16.2 0.0 collective-permute-start.3
  16.2 2.6 %collective-permute-done.2.x1_ref = f32[168,128]{1,0:T(8,128)S(1)} collective-permute-done((f32[168,128]{1,0:T(8,128)S(1)}, f32[168,128]{1,0:T(8,128)S(1)}, u32[]{:S(2)}, u32[]{:S(2)}) %collective-permute-start.2) | collective-permute-done | bytes 86048 | tf_op jit(solution)/shard_map/ppermute | solution.py:553
  18.8 0.0 collective-permute-done.3.x0_ref
  18.8 2.8 %shard_map.98 = (f32[16,16,8,128]{3,2,1,0:T(8,128)}, f32[16,4,256]{2,1,0:T(4,128)}, f32[16,4,64]{2,1,0:T(4,128)}) custom-call(f32[16,16,8,128]{3,2,1,0:T(8,128)S(1)} %bitcast.13, s32[4,1024]{1,0:T(4,128)S(1)} %copy-done.1, f32[2,160,128]{2,1,0:T(8,128)S(1)} %get-tuple-element.19.joined_ref, f32[104,128]{1,0:T(8,128)S(1)} %collective-permute-done.in1_ref.y1_ref, ...), custom_call_target="tpu_custom_call" | custom-call | flops 10000000 | bytes 1048576 | tf_op jit(solution)/shard_map/pallas_call | solution.py:607
  (3 shorter events, 0.0 us)
Async XLA Ops:
  0.6 0.7 %copy-start.1 = (s32[4,1024]{1,0:T(4,128)S(1)}, s32[4,1024]{1,0:T(4,128)}, u32[]{:S(2)}) copy-start(s32[4,1024]{1,0:T(4,128)} %cells_ref.5) | copy-start | bytes 49156
  0.6 0.8 %copy-start.3 = (f32[16,4,64]{2,1,0:T(4,128)S(1)}, f32[16,4,64]{2,1,0:T(4,128)}, u32[]{:S(2)}) copy-start(f32[16,4,64]{2,1,0:T(4,128)} %corner_ref.1) | copy-start | bytes 49156
  0.7 0.9 %copy-start.2 = (f32[16,4,256]{2,1,0:T(4,128)S(1)}, f32[16,4,256]{2,1,0:T(4,128)}, u32[]{:S(2)}) copy-start(f32[16,4,256]{2,1,0:T(4,128)} %outbox_ref.1) | copy-start | bytes 196612
  0.7 1.3 %copy-start = (f32[16,4,4096]{2,1,0:T(4,128)S(1)}, f32[16,4,4096]{2,1,0:T(4,128)}, u32[]{:S(2)}) copy-start(f32[16,4,4096]{2,1,0:T(4,128)} %param.7) | copy-start | bytes 3145732
  0.7 1.3 %copy-start.4 = (s32[4,256]{1,0:T(4,128)S(1)}, s32[4,256]{1,0:T(4,128)}, u32[]{:S(2)}) copy-start(s32[4,256]{1,0:T(4,128)} %face_cell_ref.1) | copy-start | bytes 12292
  0.7 1.2 %copy-start.5 = (s32[4,64]{1,0:T(4,128)S(1)}, s32[4,64]{1,0:T(4,128)}, u32[]{:S(2)}) copy-start(s32[4,64]{1,0:T(4,128)} %corner_cell_ref.1) | copy-start | bytes 3076
  0.7 1.2 %copy-start.6 = (s32[8,1]{0,1:T(1,128)S(1)}, s32[8,1]{0,1:T(1,128)}, u32[]{:S(2)}) copy-start(s32[8,1]{0,1:T(1,128)} %param.13) | copy-start | bytes 100
  3.0 6.3 %collective-permute-start = (f32[104,128]{1,0:T(8,128)S(1)}, f32[104,128]{1,0:T(8,128)S(1)}, u32[]{:S(2)}, u32[]{:S(2)}) collective-permute-start(f32[104,128]{1,0:T(8,128)S(1)} %get-tuple-element.16), channel_id=1, source_target_pairs={{0,7},{1,2},{2,1},{3,4},{4,3},{5,6},{6,5},{7,0},{8,15},{9,10},{10,... | collective-permute-start | bytes 159752 | tf_op jit(solution)/shard_map/ppermute | solution.py:553
  7.0 4.1 %collective-permute-start.1 = (f32[104,128]{1,0:T(8,128)S(1)}, f32[104,128]{1,0:T(8,128)S(1)}, u32[]{:S(2)}, u32[]{:S(2)}) collective-permute-start(f32[104,128]{1,0:T(8,128)S(1)} %get-tuple-element.17), channel_id=1, source_target_pairs={{0,1},{1,0},{2,3},{3,2},{4,5},{5,4},{6,7},{7,6},{8,9},{9,8},{10,11... | collective-permute-start | bytes 159752 | tf_op jit(solution)/shard_map/ppermute | solution.py:553
  11.2 7.6 %collective-permute-start.2 = (f32[168,128]{1,0:T(8,128)S(1)}, f32[168,128]{1,0:T(8,128)S(1)}, u32[]{:S(2)}, u32[]{:S(2)}) collective-permute-start(f32[168,128]{1,0:T(8,128)S(1)} %get-tuple-element.20), channel_id=1, source_target_pairs={{0,120},{8,16},{16,8},{24,32},{32,24},{40,48},{48,40},{56,64},{64,... | collective-permute-start | bytes 258056 | tf_op jit(solution)/shard_map/ppermute | solution.py:553
  16.2 2.6 %collective-permute-start.3 = (f32[168,128]{1,0:T(8,128)S(1)}, f32[168,128]{1,0:T(8,128)S(1)}, u32[]{:S(2)}, u32[]{:S(2)}) collective-permute-start(f32[168,128]{1,0:T(8,128)S(1)} %get-tuple-element.21), channel_id=1, source_target_pairs={{0,8},{8,0},{16,24},{24,16},{32,40},{40,32},{48,56},{56,48},{64,72... | collective-permute-start | bytes 258056 | tf_op jit(solution)/shard_map/ppermute | solution.py:553

commit v3 on v2

--- a/solution.py
+++ b/solution.py
@@ -15,7 +15,8 @@
 YY = 20
 YP = 24
 Y_ROWS = 104
-X_ROWS = 168
+Y_STATES = 48
+X_ROWS = 160
 X_STATES = 112
 time_step = 0.1
 gravity = 1.0
@@ -41,12 +42,10 @@
     return mass, carried, affine
 
 
-def placed(rows, width, cell, weights, wrap=None, row=None):
+def placed(rows, width, cell, weights, row=None):
     if row is None:
         row = lax.broadcasted_iota(jnp.int32, (rows, width), 0)
     step = row - cell
-    if wrap is not None:
-        step = jnp.where(step > wrap // 2, step - wrap, jnp.where(step < -wrap // 2, step + wrap, step))
     low, mid, high = weights
     zero = jnp.zeros((rows, width), F32)
     is_low, is_high = step == -1, step == 1
@@ -107,9 +106,8 @@
     return (slot < counts).astype(F32)
 
 
-def deposit_residents(res_ref, count_ref, terms_ref, total_ref, first, last):
+def deposit_residents(res_ref, count_ref, terms_ref, shift_ref, total_ref, first, last):
     row = lax.broadcasted_iota(jnp.int32, (8, 128), 0)
-    keep = row < CX
     for y in range(first, last):
         state = [res_ref[c, y] for c in range(16)]
         mass, carried, affine = deposit_terms(state, resident_living(count_ref, y))
@@ -128,11 +126,8 @@
                     + pltpu.roll(sums.pop((node, c, 1)), 1, 1)
                     + pltpu.roll(sums.pop((node, c, -1)), 127, 1)
                 )
-                value = jnp.where(keep, value + pltpu.roll(value, CX, 0), 0.0)
-                if ex != 0:
-                    value = pltpu.roll(value, ex % 8, 0)
                 at = (node + 2) * 8
-                total_ref[c, at : at + 8, :] += value
+                shift_ref[ex + 1, c, at : at + 8, :] = value
 
         for y in range(first, last):
             term = [terms_ref[y, k] for k in range(13)]
@@ -163,6 +158,15 @@
             finish_node(y - 1)
         finish_node(last - 1)
         finish_node(last)
+    for node in range(first - 1, last + 1):
+        at = (node + 2) * 8
+        for c in range(4):
+            value = total_ref[c, at : at + 8, :]
+            for ex in STEPS:
+                low = at - 2 - ex
+                both = shift_ref[ex + 1, c, low : low + 8, :] + shift_ref[ex + 1, c, low + 4 : low + 12, :]
+                value = value + jnp.where((row >= 2 + ex) & (row < 2 + ex + CX), both, 0.0)
+            total_ref[c, at : at + 8, :] = value
 
 
 def decode(cells):
@@ -207,7 +211,7 @@
         product = scatter_product(jnp.concatenate(lines, axis=0), *depth)
         for c in range(4):
             for e in STEPS:
-                row = ((CX if g == 0 else -1) + e) % 8
+                row = (CX if g == 0 else -1) + e + 2
                 for start, count in chunks:
                     at = (3 * c + e + 1) * rows + start
                     total_ref[c, pl.ds(row_nodes[start] * 8 + row, count, stride=8), :] += product[
@@ -219,8 +223,8 @@
     mark_ref[...] = jnp.zeros_like(mark_ref)
 
 
-def edge_kernel(mark_ref, count_ref, res_ref, cells_ref, outbox_ref, corner_ref, face_cell_ref,
-                corner_cell_ref, msg0_ref, msg1_ref, ahead_ref, total_ref, wide_ref, terms_ref, stage_ref):
+def leave_kernel(mark_ref, count_ref, outbox_ref, corner_ref, face_cell_ref, corner_cell_ref,
+                 total_ref, stage_ref, ahead_ref, wide_ref):
     total_ref[...] = jnp.zeros_like(total_ref)
 
     def count(k, width):
@@ -246,16 +250,16 @@
         for side in range(2):
             pair = join_pairs(corner, side, side + 2)
             if c < 16:
-                stage_ref[side, 48 + c : 49 + c, :] = face[2 + side : 3 + side, 0:128]
-                stage_ref[side, 64 + c : 65 + c, :] = face[2 + side : 3 + side, 128:256]
-                stage_ref[side, 80 + c : 81 + c, :] = pair
+                stage_ref[side, c : 1 + c, :] = face[2 + side : 3 + side, 0:128]
+                stage_ref[side, 16 + c : 17 + c, :] = face[2 + side : 3 + side, 128:256]
+                stage_ref[side, 32 + c : 33 + c, :] = pair
                 ahead_ref[side, c : c + 1, :] = face[side : side + 1, 0:128]
                 ahead_ref[side, 16 + c : 17 + c, :] = face[side : side + 1, 128:256]
             else:
-                stage_ref[side, 96:97, :] = face[2 + side : 3 + side, 0:128]
-                stage_ref[side, 97:98, :] = face[2 + side : 3 + side, 128:256]
-                stage_ref[side, 98:99, :] = pair
-                stage_ref[side, 99:104, :] = jnp.zeros((5, 128), F32)
+                stage_ref[side, 48:49, :] = face[2 + side : 3 + side, 0:128]
+                stage_ref[side, 49:50, :] = face[2 + side : 3 + side, 128:256]
+                stage_ref[side, 50:51, :] = pair
+                stage_ref[side, 51:56, :] = jnp.zeros((5, 128), F32)
                 ahead_ref[side, 32:33, :] = face[side : side + 1, 0:128]
                 ahead_ref[side, 33:34, :] = face[side : side + 1, 128:256]
                 ahead_ref[side, 34:40, :] = jnp.zeros((6, 128), F32)
@@ -277,7 +281,7 @@
     weights = [spline(state[axis]) for axis in range(3)]
     for g in range(2):
         depth = placed(NZ, MIG, row_of(cell_z, g), [row_of(w, g) for w in weights[2]])
-        across, across_moment = placed(8, MIG, row_of(cell_x, g), [row_of(w, g) for w in weights[0]], 8)
+        across, across_moment = placed(8, MIG, row_of(cell_x, g) + 2, [row_of(w, g) for w in weights[0]])
         lines = []
         zero = jnp.zeros((8, MIG), F32)
         for c in range(4):
@@ -299,8 +303,12 @@
                 line = (3 * c + e + 1) * 8
                 total_ref[c, at : at + 8, :] += product[line : line + 8, :]
 
-    deposit_residents(res_ref, cells_ref, terms_ref, total_ref, 0, 2)
-    deposit_residents(res_ref, cells_ref, terms_ref, total_ref, CY - 2, CY)
+
+def edge_kernel(res_ref, cells_ref, states_ref, before_ref, msg0_ref, msg1_ref, total_ref,
+                terms_ref, shift_ref, stage_ref):
+    total_ref[...] = before_ref[...]
+    deposit_residents(res_ref, cells_ref, terms_ref, shift_ref, total_ref, 0, 2)
+    deposit_residents(res_ref, cells_ref, terms_ref, shift_ref, total_ref, CY - 2, CY)
 
     for side in range(2):
         for pair in range(2):
@@ -310,16 +318,17 @@
                     total_ref[2 * pair, at : at + 8, :], total_ref[2 * pair + 1, at : at + 8, :]
                 )
     parity = lax.axis_index("gy") % 2
-    msg0_ref[...] = stage_ref[parity]
-    msg1_ref[...] = stage_ref[1 - parity]
-
-
-def inner_kernel(res_ref, cells_ref, before_ref, wide_ref, grid_ref, total_ref, terms_ref):
+    for msg_ref, side in ((msg0_ref, parity), (msg1_ref, 1 - parity)):
+        msg_ref[0:Y_STATES, :] = stage_ref[side]
+        msg_ref[Y_STATES:Y_ROWS, :] = states_ref[side]
+
+
+def inner_kernel(res_ref, cells_ref, before_ref, wide_ref, grid_ref, total_ref, terms_ref, shift_ref):
     total_ref[...] = before_ref[...]
     deposit_wide(
         [wide_ref[c] for c in range(16)], wide_ref[16], total_ref, list(range(3, 19)), [(0, 14)]
     )
-    deposit_residents(res_ref, cells_ref, terms_ref, total_ref, 2, CY - 2)
+    deposit_residents(res_ref, cells_ref, terms_ref, shift_ref, total_ref, 2, CY - 2)
     for pair in range(2):
         for yy in range(YY):
             at = yy * 8
@@ -342,10 +351,9 @@
     for side in range(2):
         for pair in range(2):
             for j in range(3):
-                row = (3 + j) if side == 0 else (6 + j) % 8
+                row = (5 + j) if side == 0 else j
                 at = (3 * pair + j) * 18
                 stage_ref[side, at : at + 18, :] = joined_ref[pair, pl.ds(8 + row, 18, stride=8), :]
-        stage_ref[side, 108:112, :] = jnp.zeros((4, 128), F32)
         stage_ref[side, X_STATES : X_STATES + 32, :] = ahead_ref[side, 0:32, :]
         from_below, from_above = got_ref[0, 80:96, :], got_ref[1, 80:96, :]
         cell_below, cell_above = got_ref[0, 96:104, :], got_ref[1, 96:104, :]
@@ -356,9 +364,9 @@
             states = jnp.where(low, swap_half(from_below), from_above)
             cells = jnp.where(low[0:8], swap_half(cell_below), cell_above)
         stage_ref[side, X_STATES + 32 : X_STATES + 48, :] = states
-        stage_ref[side, X_STATES + 48 : X_STATES + 56, :] = jnp.zeros((8, 128), F32)
-        stage_ref[side, X_STATES + 48 : X_STATES + 50, :] = ahead_ref[side, 32:34, :]
-        stage_ref[side, X_STATES + 50 : X_STATES + 51, :] = cells[2:3, :]
+        stage_ref[side, 108:110, :] = ahead_ref[side, 32:34, :]
+        stage_ref[side, 110:111, :] = cells[2:3, :]
+        stage_ref[side, 111:112, :] = jnp.zeros((1, 128), F32)
     parity = lax.axis_index("gx") % 2
     msg0_ref[...] = stage_ref[parity]
     msg1_ref[...] = stage_ref[1 - parity]
@@ -396,11 +404,15 @@
 
 
 def finished(state, living, velocity, slopes):
-    out = [living * (state[k] + time_step * velocity[k]) for k in range(3)]
-    out += [living * velocity[k] for k in range(3)]
+    out = [living * state[k] + (0.25 * time_step) * velocity[k] for k in range(3)]
+    out += [0.25 * velocity[k] for k in range(3)]
     for i in range(3):
-        out += [living * (4.0 * (slopes[i][k] - state[k] * velocity[i])) for k in range(3)]
+        out += [slopes[i][k] - state[k] * velocity[i] for k in range(3)]
     return out + [living * state[15]]
+
+
+def both(first, second):
+    return jnp.concatenate([first, second], axis=0)
 
 
 def last_kernel(res_ref, cells_ref, joined_ref, y1_ref, y0_ref, x1_ref, x0_ref,
@@ -417,7 +429,7 @@
     for side in range(2):
         for pair in range(2):
             for j in range(3):
-                row = ((3 + j) if side == 0 else (6 + j) % 8) ^ 4
+                row = (1 + j) if side == 0 else (4 + j)
                 at = (3 * pair + j) * 18
                 grid_ref[pair, pl.ds(8 + row, 18, stride=8), :] += got_x_ref[side, at : at + 18, :]
 
@@ -431,24 +443,22 @@
         first = grid_ref[0, yy * 8 : yy * 8 + 8, :]
         second = grid_ref[1, yy * 8 : yy * 8 + 8, :]
         first_swap, second_swap = swap_half(first), swap_half(second)
-        mass = jnp.maximum(jnp.where(low, first, first_swap), mass_floor)
+        share = 1.0 / (0.25 * jnp.maximum(jnp.where(low, first, first_swap), mass_floor))
         momentum = (
             jnp.where(low, first_swap, first),
             jnp.where(low, second, second_swap),
             jnp.where(low, second_swap, second),
         )
         for i in range(3):
-            value = momentum[i] / mass
+            value = (0.25 * momentum[i]) * share
             if i == 2:
                 value = value - time_step * gravity
-            value = jnp.where(inside, value, 0.0)
-            vel_ref[i, yy * 8 : yy * 8 + 8, :] = value
+            vel_ref[i, yy * 8 : yy * 8 + 8, :] = jnp.where(inside, value, 0.0)
+    for yy in range(1, CY + 3):
+        for i in range(3):
             for ex in STEPS:
-                near = jnp.where(
-                    upper,
-                    pltpu.roll(value, (-ex) % 8, 0) if ex != 0 else value,
-                    pltpu.roll(value, (CX - ex) % 8, 0),
-                )
+                at = yy * 8 + ex
+                near = jnp.where(upper, vel_ref[i, at + 2 : at + 10, :], vel_ref[i, at - 2 : at + 6, :])
                 near_ref[ex + 1, 1, i, yy - 1] = near
                 near_ref[ex + 1, 0, i, yy - 1] = pltpu.roll(near, 1, 1)
                 near_ref[ex + 1, 2, i, yy - 1] = pltpu.roll(near, 127, 1)
@@ -458,6 +468,8 @@
         state = [res_ref[c, y] for c in range(16)]
         living = resident_living(cells_ref, y)
         weights = [spline(state[axis]) for axis in range(3)]
+        scale = 4.0 * living
+        weights[0] = [scale * value for value in weights[0]]
         velocity, slopes = [], []
         for i in range(3):
             by_x = []
@@ -493,48 +505,59 @@
             )
             copies[-1].start()
 
-    for side in range(2):
-        def wide_row(k):
-            return jnp.concatenate([got_x_ref[side, a : a + 1, :] for a in k], axis=1)
-
-        base = X_STATES
-        state = [wide_row((base + c, base + 16 + c, base + 32 + c)) for c in range(16)]
-        number = wide_row((base + 48, base + 49, base + 50)).astype(jnp.int32)
+    def rows_of(got_ref, lines):
+        return jnp.concatenate(
+            [both(got_ref[0, a : a + 1, :], got_ref[1, a : a + 1, :]) for a in lines], axis=1
+        )
+
+    def prepared(got_ref, lines, cell_lines):
+        state = [rows_of(got_ref, [a + c for a in lines]) for c in range(16)]
+        number = rows_of(got_ref, cell_lines).astype(jnp.int32)
         living = (number >= 0).astype(F32)
         weights = [spline(state[axis]) for axis in range(3)]
-        depth = placed(NZ, WIDE, number % NZ, weights[2])
-        across, across_moment = placed(YP, WIDE, (number // NZ) % CY + 2, weights[1])
-        lines = []
-        for i in range(3):
-            for e in STEPS:
-                at = ((0 if side == 0 else CX - 1) + e) % 8
-                lines.append(vel_ref[i, pl.ds(at, YP, stride=8), :])
-        product = gather_product(jnp.concatenate(lines, axis=0), *depth)
-        velocity, slopes = contract(product, YP, WIDE, weights[0], across, across_moment, 0, 1)
-        for c, value in enumerate(finished(state, living, velocity, slopes)):
-            face_out_ref[c, side : side + 1, :] = value[:, 0:MIG]
-            corner_out_ref[c, 2 * side : 2 * side + 1, :] = value[:, MIG : MIG + CORNER]
-            corner_out_ref[c, 2 * side + 1 : 2 * side + 2, :] = value[:, MIG + CORNER : WIDE]
-
+        return state, number, living, weights
+
+    def gathered(side, nodes, rows, width, number, across_cell, weights, scale, normal_axis, across_axis):
+        picked = [[row_of(value, side) for value in weights[axis]] for axis in range(3)]
+        depth = placed(NZ, width, row_of(number % NZ, side), picked[2])
+        across, across_moment = placed(rows, width, row_of(across_cell, side), picked[across_axis])
+        product = gather_product(jnp.concatenate(nodes, axis=0), *depth)
+        normal = [row_of(scale, side) * value for value in picked[normal_axis]]
+        return contract(product, rows, width, normal, across, across_moment, normal_axis, across_axis)
+
+    def joined_sides(parts):
+        velocity = [both(parts[0][0][i], parts[1][0][i]) for i in range(3)]
+        slopes = [[both(parts[0][1][i][k], parts[1][1][i][k]) for k in range(3)] for i in range(3)]
+        return velocity, slopes
+
+    state, number, living, weights = prepared(
+        got_x_ref, (X_STATES, X_STATES + 16, X_STATES + 32), (108, 109, 110)
+    )
+    parts = []
     for side in range(2):
-        def face_row(k):
-            return jnp.concatenate([got_y_ref[side, a : a + 1, :] for a in k], axis=1)
-
-        state = [face_row((48 + c, 64 + c)) for c in range(16)]
-        number = face_row((96, 97)).astype(jnp.int32)
-        living = (number >= 0).astype(F32)
-        weights = [spline(state[axis]) for axis in range(3)]
-        depth = placed(NZ, MIG, number % NZ, weights[2])
-        across, across_moment = placed(8, MIG, jnp.maximum(number, 0) // (CY * NZ), weights[0], 8)
-        lines = []
-        for i in range(3):
-            for e in STEPS:
-                at = ((0 if side == 0 else CY - 1) + 2 + e) * 8
-                lines.append(vel_ref[i, at : at + 8, :])
-        product = gather_product(jnp.concatenate(lines, axis=0), *depth)
-        velocity, slopes = contract(product, 8, MIG, weights[1], across, across_moment, 1, 0)
-        for c, value in enumerate(finished(state, living, velocity, slopes)):
-            face_out_ref[c, 2 + side : 3 + side, :] = value
+        first = (0 if side == 0 else CX - 1) + 2
+        nodes = [vel_ref[i, pl.ds(first + e, YP, stride=8), :] for i in range(3) for e in STEPS]
+        parts.append(
+            gathered(side, nodes, YP, WIDE, number, (number // NZ) % CY + 2, weights, 4.0 * living, 0, 1)
+        )
+    for c, value in enumerate(finished(state, living, *joined_sides(parts))):
+        face_out_ref[c, 0:2, :] = value[:, 0:MIG]
+        for side in range(2):
+            corner_out_ref[c, 2 * side : 2 * side + 1, :] = row_of(value, side)[:, MIG : MIG + CORNER]
+            corner_out_ref[c, 2 * side + 1 : 2 * side + 2, :] = row_of(value, side)[:, MIG + CORNER : WIDE]
+
+    state, number, living, weights = prepared(got_y_ref, (48, 64), (96, 97))
+    parts = []
+    for side in range(2):
+        first = (0 if side == 0 else CY - 1) + 2
+        nodes = [
+            vel_ref[i, (first + e) * 8 : (first + e) * 8 + 8, :] for i in range(3) for e in STEPS
+        ]
+        parts.append(
+            gathered(side, nodes, 8, MIG, number, number // (CY * NZ) + 2, weights, 4.0 * living, 1, 0)
+        )
+    for c, value in enumerate(finished(state, living, *joined_sides(parts))):
+        face_out_ref[c, 2:4, :] = value
 
     copies.append(pltpu.make_async_copy(face_out_ref, face_out_hbm, sems.at[4]))
     copies.append(pltpu.make_async_copy(corner_out_ref, corner_out_hbm, sems.at[5]))
@@ -576,14 +599,22 @@
 def body(residents, cell_count, outbox, corner_box, face_cell, corner_cell, mig_count):
     res = residents.reshape(16, CX, CY, 2, 128).transpose(0, 2, 3, 1, 4).reshape(16, CY, 8, 128)
     (mark,) = call(open_kernel, [], VMEM, [(8, 128)], [], 10_000_000_000)()
-    msg0, msg1, ahead, total, wide = call(
+    left, states, ahead, wide = call(
+        leave_kernel,
+        [VMEM] * 6,
+        VMEM,
+        [(4, YP * 8, 128), (2, Y_ROWS - Y_STATES, 128), (2, 40, 128), (17, 2, WIDE)],
+        [],
+        10_000_000,
+    )(mark, mig_count.reshape(1, 8), outbox, corner_box, face_cell, corner_cell)
+    msg0, msg1, total = call(
         edge_kernel,
-        [VMEM] * 8,
+        [VMEM] * 4,
         VMEM,
-        [(Y_ROWS, 128), (Y_ROWS, 128), (2, 40, 128), (4, YP * 8, 128), (17, 2, WIDE)],
-        [scratch((CY, 22, 8, 128)), scratch((2, Y_ROWS, 128))],
+        [(Y_ROWS, 128), (Y_ROWS, 128), (4, YP * 8, 128)],
+        [scratch((CY, 22, 8, 128)), scratch((3, 4, YP * 8, 128)), scratch((2, Y_STATES, 128))],
         10_000_000,
-    )(mark, mig_count.reshape(1, 8), res, cell_count, outbox, corner_box, face_cell, corner_cell)
+    )(res, cell_count, states, left)
     y0 = swapped(msg0, "gy", 0)
     y1 = swapped(msg1, "gy", 1)
     (grid,) = call(
@@ -591,7 +622,7 @@
         [VMEM] * 4,
         VMEM,
         [(2, YY * 8, 128)],
-        [scratch((4, YP * 8, 128)), scratch((CY, 22, 8, 128))],
+        [scratch((4, YP * 8, 128)), scratch((CY, 22, 8, 128)), scratch((3, 4, YP * 8, 128))],
         10_000_000,
     )(res, cell_count, total, wide)
     joined, msg0, msg1 = call(

time: 21.7 us -> 21.2 us (0.977)
  local copies, waits for them, and re-layouts: 1.24 us -> 0.8 us
    unnamed x14, local copies, waits for them, and re-layouts: 1.24 us -> 0.8 us
    pallas_call x1 -> x2, Pallas kernels: 1.09 us -> 1.27 us  [the longest x1 0.77 us: body(): call(leave_kernel, [VMEM] * 6, VMEM, [(4, YP * 8, 128), (2, Y_ROWS - Y_ST...]
where the time goes in v3:
time: 21.2 us; the launch traced here: 21.1 us
  starting transfers between devices  8.97 us (42%)
  Pallas kernels  5.38 us (25%)
  waiting for transfers between devices  5.19 us (24%)
  local copies, waits for them, and re-layouts  0.8 us (4%)
  between operations  0.72 us (3%)
    ppermute x4, starting transfers between devices, swapped(): lax.ppermute(value, axis, [(i, partner(i, phase, count)) for i in range(c...  8.97 us
    ppermute x4, waiting for transfers between devices, swapped(): lax.ppermute(value, axis, [(i, partner(i, phase, count)) for i in range(c...  5.19 us
    pallas_call x1, Pallas kernels, body(): call(last_kernel, [VMEM] * 7, HBM, [(16, CY, 8, 128), (16, 4, MIG), (16,...  2.55 us
    pallas_call x1, Pallas kernels, body(): call(inner_kernel, [VMEM] * 4, VMEM, [(2, YY * 8, 128)], [scratch((4, YP...  1.46 us
    unnamed x14, local copies, waits for them, and re-layouts  0.8 us
    pallas_call x1, Pallas kernels, body(): call(leave_kernel, [VMEM] * 6, VMEM, [(4, YP * 8, 128), (2, Y_ROWS - Y_ST...  0.77 us
    pallas_call x1, Pallas kernels, body(): call(edge_kernel, [VMEM] * 4, VMEM, [(Y_ROWS, 128), (Y_ROWS, 128), (4, YP...  0.49 us
  transfers between devices with their start and end apart: 4, of which 3 were waited for; matrix products, arithmetic and copies ran while one was open for 0% of the time, Pallas kernels for 7%

profile of v3, /device:TPU:0, one launch (start us, length us, event | category | flops | bytes accessed | tf_op | source)
XLA Modules:
  0.0 21.1 jit_solution(9791006878557450789)
XLA Ops:
  0.6 0.0 copy-start.3
  0.6 0.0 copy-start.2
  0.7 0.0 copy-start.4
  0.7 0.0 copy-start.5
  0.7 0.0 copy-start
  0.7 0.0 copy-start.1
  0.7 0.0 copy-start.6
  0.7 0.7 %copy-done.3 = f32[16,4,64]{2,1,0:T(4,128)S(1)} copy-done((f32[16,4,64]{2,1,0:T(4,128)S(1)}, f32[16,4,64]{2,1,0:T(4,128)}, u32[]{:S(2)}) %copy-start.3) | copy-done | bytes 16408
  1.4 0.1 copy-done.2
  1.5 0.0 copy-done.4
  1.5 0.0 copy-done.6
  1.5 0.8 %shard_map.95 = (f32[4,192,128]{2,1,0:T(8,128)S(1)}, f32[2,56,128]{2,1,0:T(8,128)S(1)}, f32[2,40,128]{2,1,0:T(8,128)S(1)}, f32[17,2,384]{2,1,0:T(2,128)S(1)}) custom-call(f32[8,128]{1,0:T(8,128)S(1)} %shard_map.94.mark_ref, s32[1,8]{1,0:T(1,128)S(1)} %bitcast.14, f32[16,4,256]{2,1,0:T(4,128)S(1)} %copy-done.2, f32[16,4,64]{2,1,0:T(4,128)S(1)} %copy-done.3, ...), custom_call_target="tpu_custom_call" | custom-call | flops 10000000 | bytes 1048576 | tf_op jit(solution)/shard_map/pallas_call | solution.py:602
  2.3 0.5 %shard_map.96 = (f32[104,128]{1,0:T(8,128)S(1)}, f32[104,128]{1,0:T(8,128)S(1)}, f32[4,192,128]{2,1,0:T(8,128)S(1)}) custom-call(f32[16,16,8,128]{3,2,1,0:T(8,128)S(1)} %bitcast.11, s32[4,1024]{1,0:T(4,128)S(1)} %copy-done.1, f32[2,56,128]{2,1,0:T(8,128)S(1)} %get-tuple-element.16.states_ref, f32[4,192,128]{2,1,0:T(8,128)S(1)} %get-tuple-element.17.before_ref), custom_call_target="tpu_custom_call" | custom-call | flops 10000000 | bytes 1048576 | tf_op jit(solution)/shard_map/pallas_call | solution.py:610
  2.8 3.9 %collective-permute-start = (f32[104,128]{1,0:T(8,128)S(1)}, f32[104,128]{1,0:T(8,128)S(1)}, u32[]{:S(2)}, u32[]{:S(2)}) collective-permute-start(f32[104,128]{1,0:T(8,128)S(1)} %get-tuple-element.20), channel_id=1, source_target_pairs={{0,7},{1,2},{2,1},{3,4},{4,3},{5,6},{6,5},{7,0},{8,15},{9,10},{10,... | collective-permute-start | bytes 159752 | tf_op jit(solution)/shard_map/ppermute | solution.py:576
  6.7 0.0 collective-permute-start.1
  6.7 1.5 %shard_map.97.grid_ref = f32[2,160,128]{2,1,0:T(8,128)S(1)} custom-call(f32[16,16,8,128]{3,2,1,0:T(8,128)S(1)} %bitcast.12, s32[4,1024]{1,0:T(4,128)S(1)} %copy-done.1, f32[4,192,128]{2,1,0:T(8,128)S(1)} %get-tuple-element.18.before_ref, f32[17,2,384]{2,1,0:T(2,128)S(1)} %get-tuple-element.19.wide_ref), custom_call_target="tpu_custom_call" | custom-call | flops 10000000 | bytes 1048576 | tf_op jit(solution)/shard_map/pallas_call | solution.py:620
  8.2 0.9 %collective-permute-done.in1_ref.y1_ref = f32[104,128]{1,0:T(8,128)S(1)} collective-permute-done((f32[104,128]{1,0:T(8,128)S(1)}, f32[104,128]{1,0:T(8,128)S(1)}, u32[]{:S(2)}, u32[]{:S(2)}) %collective-permute-start) | collective-permute-done | bytes 53280 | tf_op jit(solution)/shard_map/ppermute | solution.py:576
  9.1 1.7 %collective-permute-done.1.in0_ref.y0_ref = f32[104,128]{1,0:T(8,128)S(1)} collective-permute-done((f32[104,128]{1,0:T(8,128)S(1)}, f32[104,128]{1,0:T(8,128)S(1)}, u32[]{:S(2)}, u32[]{:S(2)}) %collective-permute-start.1) | collective-permute-done | bytes 53280 | tf_op jit(solution)/shard_map/ppermute | solution.py:576
  10.9 0.1 shard_map.98
  11.0 5.0 %collective-permute-start.2 = (f32[160,128]{1,0:T(8,128)S(1)}, f32[160,128]{1,0:T(8,128)S(1)}, u32[]{:S(2)}, u32[]{:S(2)}) collective-permute-start(f32[160,128]{1,0:T(8,128)S(1)} %get-tuple-element.24), channel_id=1, source_target_pairs={{0,120},{8,16},{16,8},{24,32},{32,24},{40,48},{48,40},{56,64},{64,... | collective-permute-start | bytes 245768 | tf_op jit(solution)/shard_map/ppermute | solution.py:576
  16.0 0.0 collective-permute-start.3
  16.0 2.5 %collective-permute-done.2.x1_ref = f32[160,128]{1,0:T(8,128)S(1)} collective-permute-done((f32[160,128]{1,0:T(8,128)S(1)}, f32[160,128]{1,0:T(8,128)S(1)}, u32[]{:S(2)}, u32[]{:S(2)}) %collective-permute-start.2) | collective-permute-done | bytes 81952 | tf_op jit(solution)/shard_map/ppermute | solution.py:576
  18.5 0.0 collective-permute-done.3.x0_ref
  18.5 2.5 %shard_map.99 = (f32[16,16,8,128]{3,2,1,0:T(8,128)}, f32[16,4,256]{2,1,0:T(4,128)}, f32[16,4,64]{2,1,0:T(4,128)}) custom-call(f32[16,16,8,128]{3,2,1,0:T(8,128)S(1)} %bitcast.13, s32[4,1024]{1,0:T(4,128)S(1)} %copy-done.1, f32[2,160,128]{2,1,0:T(8,128)S(1)} %get-tuple-element.23.joined_ref, f32[104,128]{1,0:T(8,128)S(1)} %collective-permute-done.in1_ref.y1_ref, ...), custom_call_target="tpu_custom_call" | custom-call | flops 10000000 | bytes 1048576 | tf_op jit(solution)/shard_map/pallas_call | solution.py:638
  (4 shorter events, 0.0 us)
Async XLA Ops:
  0.6 0.8 %copy-start.3 = (f32[16,4,64]{2,1,0:T(4,128)S(1)}, f32[16,4,64]{2,1,0:T(4,128)}, u32[]{:S(2)}) copy-start(f32[16,4,64]{2,1,0:T(4,128)} %corner_ref.1) | copy-start | bytes 49156
  0.6 0.8 %copy-start.2 = (f32[16,4,256]{2,1,0:T(4,128)S(1)}, f32[16,4,256]{2,1,0:T(4,128)}, u32[]{:S(2)}) copy-start(f32[16,4,256]{2,1,0:T(4,128)} %outbox_ref.1) | copy-start | bytes 196612
  0.7 0.8 %copy-start.4 = (s32[4,256]{1,0:T(4,128)S(1)}, s32[4,256]{1,0:T(4,128)}, u32[]{:S(2)}) copy-start(s32[4,256]{1,0:T(4,128)} %face_cell_ref.1) | copy-start | bytes 12292
  0.7 0.8 %copy-start.5 = (s32[4,64]{1,0:T(4,128)S(1)}, s32[4,64]{1,0:T(4,128)}, u32[]{:S(2)}) copy-start(s32[4,64]{1,0:T(4,128)} %corner_cell_ref.1) | copy-start | bytes 3076
  0.7 1.6 %copy-start = (f32[16,4,4096]{2,1,0:T(4,128)S(1)}, f32[16,4,4096]{2,1,0:T(4,128)}, u32[]{:S(2)}) copy-start(f32[16,4,4096]{2,1,0:T(4,128)} %param.7) | copy-start | bytes 3145732
  0.7 1.6 %copy-start.1 = (s32[4,1024]{1,0:T(4,128)S(1)}, s32[4,1024]{1,0:T(4,128)}, u32[]{:S(2)}) copy-start(s32[4,1024]{1,0:T(4,128)} %cells_ref.5) | copy-start | bytes 49156
  0.7 0.8 %copy-start.6 = (s32[8,1]{0,1:T(1,128)S(1)}, s32[8,1]{0,1:T(1,128)}, u32[]{:S(2)}) copy-start(s32[8,1]{0,1:T(1,128)} %param.13) | copy-start | bytes 100
  2.8 6.3 %collective-permute-start = (f32[104,128]{1,0:T(8,128)S(1)}, f32[104,128]{1,0:T(8,128)S(1)}, u32[]{:S(2)}, u32[]{:S(2)}) collective-permute-start(f32[104,128]{1,0:T(8,128)S(1)} %get-tuple-element.20), channel_id=1, source_target_pairs={{0,7},{1,2},{2,1},{3,4},{4,3},{5,6},{6,5},{7,0},{8,15},{9,10},{10,... | collective-permute-start | bytes 159752 | tf_op jit(solution)/shard_map/ppermute | solution.py:576
  6.7 4.1 %collective-permute-start.1 = (f32[104,128]{1,0:T(8,128)S(1)}, f32[104,128]{1,0:T(8,128)S(1)}, u32[]{:S(2)}, u32[]{:S(2)}) collective-permute-start(f32[104,128]{1,0:T(8,128)S(1)} %get-tuple-element.21), channel_id=1, source_target_pairs={{0,1},{1,0},{2,3},{3,2},{4,5},{5,4},{6,7},{7,6},{8,9},{9,8},{10,11... | collective-permute-start | bytes 159752 | tf_op jit(solution)/shard_map/ppermute | solution.py:576
  11.0 7.6 %collective-permute-start.2 = (f32[160,128]{1,0:T(8,128)S(1)}, f32[160,128]{1,0:T(8,128)S(1)}, u32[]{:S(2)}, u32[]{:S(2)}) collective-permute-start(f32[160,128]{1,0:T(8,128)S(1)} %get-tuple-element.24), channel_id=1, source_target_pairs={{0,120},{8,16},{16,8},{24,32},{32,24},{40,48},{48,40},{56,64},{64,... | collective-permute-start | bytes 245768 | tf_op jit(solution)/shard_map/ppermute | solution.py:576
  16.0 2.5 %collective-permute-start.3 = (f32[160,128]{1,0:T(8,128)S(1)}, f32[160,128]{1,0:T(8,128)S(1)}, u32[]{:S(2)}, u32[]{:S(2)}) collective-permute-start(f32[160,128]{1,0:T(8,128)S(1)} %get-tuple-element.25), channel_id=1, source_target_pairs={{0,8},{8,0},{16,24},{24,16},{32,40},{40,32},{48,56},{56,48},{64,72... | collective-permute-start | bytes 245768 | tf_op jit(solution)/shard_map/ppermute | solution.py:576

commit v4 on v3

--- a/solution.py
+++ b/solution.py
@@ -372,16 +372,22 @@
     msg1_ref[...] = stage_ref[1 - parity]
 
 
-def gather_product(nodes, depth_plain, depth_moment):
+def both(first, second):
+    return jnp.concatenate([first, second], axis=0)
+
+
+def split_depth(depth_plain, depth_moment):
+    return split(jnp.concatenate([depth_plain, depth_moment], axis=1))
+
+
+def gather_product(nodes, coarse_depth, fine_depth):
     low = low_half(nodes.shape)
     coarse = nodes.astype(BF16).astype(F32)
     lhs = jnp.where(low, coarse, nodes - coarse).astype(BF16)
-    rhs = jnp.concatenate([depth_plain, depth_moment], axis=1)
-    coarse, fine = split(rhs)
     dims = (((1,), (0,)), ((), ()))
-    return lax.dot_general(
-        lhs, jnp.concatenate([coarse, coarse], axis=0), dims, preferred_element_type=F32
-    ) + lax.dot_general(lhs, jnp.concatenate([fine, fine], axis=0), dims, preferred_element_type=F32)
+    return lax.dot_general(lhs, both(coarse_depth, coarse_depth), dims, preferred_element_type=F32) + (
+        lax.dot_general(lhs, both(fine_depth, fine_depth), dims, preferred_element_type=F32)
+    )
 
 
 def contract(product, rows, width, normal, across, across_moment, normal_axis, across_axis):
@@ -411,16 +417,53 @@
     return out + [living * state[15]]
 
 
-def both(first, second):
-    return jnp.concatenate([first, second], axis=0)
-
-
-def last_kernel(res_ref, cells_ref, joined_ref, y1_ref, y0_ref, x1_ref, x0_ref,
-                out_hbm, face_out_hbm, corner_out_hbm, got_y_ref, got_x_ref, grid_ref, vel_ref, near_ref,
+def rows_of(got_ref, lines):
+    return jnp.concatenate([both(got_ref[0, a : a + 1, :], got_ref[1, a : a + 1, :]) for a in lines], axis=1)
+
+
+def prepared(got_ref, lines, cell_lines):
+    state = [rows_of(got_ref, [a + c for a in lines]) for c in range(16)]
+    number = rows_of(got_ref, cell_lines).astype(jnp.int32)
+    living = (number >= 0).astype(F32)
+    weights = [spline(state[axis]) for axis in range(3)]
+    return state, number, living, weights
+
+
+def laid_out(side, rows, width, number, across_cell, depth_weights, across_weights):
+    depth = placed(NZ, width, row_of(number % NZ, side), [row_of(w, side) for w in depth_weights])
+    across = placed(rows, width, row_of(across_cell, side), [row_of(w, side) for w in across_weights])
+    return split_depth(*depth), across
+
+
+def ready_kernel(res_ref, cells_ref, y1_ref, y0_ref, weights_ref, rows_ref, depth_ref, across_ref, got_ref):
+    parity = lax.axis_index("gy") % 2
+    got_ref[parity] = y1_ref[...]
+    got_ref[1 - parity] = y0_ref[...]
+    state, number, living, weights = prepared(got_ref, (48, 64), (96, 97))
+    for c in range(16):
+        rows_ref[c] = state[c]
+    rows_ref[16] = living
+    for k in range(3):
+        rows_ref[17 + k] = 4.0 * living * weights[1][k]
+    for side in range(2):
+        depth, across = laid_out(side, 8, MIG, number, number // (CY * NZ) + 2, weights[2], weights[0])
+        for k in range(2):
+            depth_ref[side, k] = depth[k]
+            across_ref[side, k] = across[k]
+    for y in range(CY):
+        living = resident_living(cells_ref, y)
+        weights = [spline(res_ref[axis, y]) for axis in range(3)]
+        scale = 4.0 * living
+        for k in range(3):
+            weights_ref[y, k] = scale * weights[0][k]
+            weights_ref[y, 3 + k] = weights[1][k]
+            weights_ref[y, 6 + k] = weights[2][k]
+        weights_ref[y, 9] = living
+
+
+def last_kernel(res_ref, joined_ref, weights_ref, rows_ref, depth_ref, across_ref, x1_ref, x0_ref,
+                out_hbm, face_out_hbm, corner_out_hbm, got_x_ref, grid_ref, vel_ref, near_ref,
                 out_ref, face_out_ref, corner_out_ref, sems):
-    parity = lax.axis_index("gy") % 2
-    got_y_ref[parity] = y1_ref[...]
-    got_y_ref[1 - parity] = y0_ref[...]
     parity = lax.axis_index("gx") % 2
     got_x_ref[parity] = x1_ref[...]
     got_x_ref[1 - parity] = x0_ref[...]
@@ -465,11 +508,9 @@
 
     copies = []
     for y in range(CY):
-        state = [res_ref[c, y] for c in range(16)]
-        living = resident_living(cells_ref, y)
-        weights = [spline(state[axis]) for axis in range(3)]
-        scale = 4.0 * living
-        weights[0] = [scale * value for value in weights[0]]
+        state = [res_ref[c, y] if c < 3 or c == 15 else None for c in range(16)]
+        living = weights_ref[y, 9]
+        weights = [[weights_ref[y, 3 * axis + k] for k in range(3)] for axis in range(3)]
         velocity, slopes = [], []
         for i in range(3):
             by_x = []
@@ -505,26 +546,6 @@
             )
             copies[-1].start()
 
-    def rows_of(got_ref, lines):
-        return jnp.concatenate(
-            [both(got_ref[0, a : a + 1, :], got_ref[1, a : a + 1, :]) for a in lines], axis=1
-        )
-
-    def prepared(got_ref, lines, cell_lines):
-        state = [rows_of(got_ref, [a + c for a in lines]) for c in range(16)]
-        number = rows_of(got_ref, cell_lines).astype(jnp.int32)
-        living = (number >= 0).astype(F32)
-        weights = [spline(state[axis]) for axis in range(3)]
-        return state, number, living, weights
-
-    def gathered(side, nodes, rows, width, number, across_cell, weights, scale, normal_axis, across_axis):
-        picked = [[row_of(value, side) for value in weights[axis]] for axis in range(3)]
-        depth = placed(NZ, width, row_of(number % NZ, side), picked[2])
-        across, across_moment = placed(rows, width, row_of(across_cell, side), picked[across_axis])
-        product = gather_product(jnp.concatenate(nodes, axis=0), *depth)
-        normal = [row_of(scale, side) * value for value in picked[normal_axis]]
-        return contract(product, rows, width, normal, across, across_moment, normal_axis, across_axis)
-
     def joined_sides(parts):
         velocity = [both(parts[0][0][i], parts[1][0][i]) for i in range(3)]
         slopes = [[both(parts[0][1][i][k], parts[1][1][i][k]) for k in range(3)] for i in range(3)]
@@ -533,29 +554,34 @@
     state, number, living, weights = prepared(
         got_x_ref, (X_STATES, X_STATES + 16, X_STATES + 32), (108, 109, 110)
     )
+    scale = 4.0 * living
     parts = []
     for side in range(2):
+        depth, across = laid_out(
+            side, YP, WIDE, number, (number // NZ) % CY + 2, weights[2], weights[1]
+        )
         first = (0 if side == 0 else CX - 1) + 2
         nodes = [vel_ref[i, pl.ds(first + e, YP, stride=8), :] for i in range(3) for e in STEPS]
-        parts.append(
-            gathered(side, nodes, YP, WIDE, number, (number // NZ) % CY + 2, weights, 4.0 * living, 0, 1)
-        )
+        product = gather_product(jnp.concatenate(nodes, axis=0), *depth)
+        normal = [row_of(scale * value, side) for value in weights[0]]
+        parts.append(contract(product, YP, WIDE, normal, *across, 0, 1))
     for c, value in enumerate(finished(state, living, *joined_sides(parts))):
         face_out_ref[c, 0:2, :] = value[:, 0:MIG]
         for side in range(2):
             corner_out_ref[c, 2 * side : 2 * side + 1, :] = row_of(value, side)[:, MIG : MIG + CORNER]
             corner_out_ref[c, 2 * side + 1 : 2 * side + 2, :] = row_of(value, side)[:, MIG + CORNER : WIDE]
 
-    state, number, living, weights = prepared(got_y_ref, (48, 64), (96, 97))
+    state = [rows_ref[c] for c in range(16)]
+    living = rows_ref[16]
     parts = []
     for side in range(2):
         first = (0 if side == 0 else CY - 1) + 2
         nodes = [
             vel_ref[i, (first + e) * 8 : (first + e) * 8 + 8, :] for i in range(3) for e in STEPS
         ]
-        parts.append(
-            gathered(side, nodes, 8, MIG, number, number // (CY * NZ) + 2, weights, 4.0 * living, 1, 0)
-        )
+        product = gather_product(jnp.concatenate(nodes, axis=0), depth_ref[side, 0], depth_ref[side, 1])
+        normal = [row_of(rows_ref[17 + k], side) for k in range(3)]
+        parts.append(contract(product, 8, MIG, normal, across_ref[side, 0], across_ref[side, 1], 1, 0))
     for c, value in enumerate(finished(state, living, *joined_sides(parts))):
         face_out_ref[c, 2:4, :] = value
 
@@ -589,7 +615,10 @@
         kernel,
         in_specs=in_specs,
         out_specs=[out_spec] * len(out_shapes),
-        out_shape=[jax.ShapeDtypeStruct(shape, F32) for shape in out_shapes],
+        out_shape=[
+            jax.ShapeDtypeStruct(shape[:-1], BF16) if shape[-1] is BF16 else jax.ShapeDtypeStruct(shape, F32)
+            for shape in out_shapes
+        ],
         scratch_shapes=scratch_shapes,
         compiler_params=pltpu.CompilerParams(vmem_limit_bytes=24 * 1024 * 1024),
         cost_estimate=pl.CostEstimate(flops=flops, bytes_accessed=1 << 20, transcendentals=0),
@@ -635,13 +664,20 @@
     )(grid, y1, y0, ahead)
     x0 = swapped(msg0, "gx", 0)
     x1 = swapped(msg1, "gx", 1)
+    weights, rows, depth, across = call(
+        ready_kernel,
+        [VMEM] * 4,
+        VMEM,
+        [(CY, 10, 8, 128), (20, 2, MIG), (2, 2, NZ, 2 * MIG, BF16), (2, 2, 8, MIG)],
+        [scratch((2, Y_ROWS, 128))],
+        10_000_000,
+    )(res, cell_count, y1, y0)
     out, face_out, corner_out = call(
         last_kernel,
-        [VMEM] * 7,
+        [VMEM] * 8,
         HBM,
         [(16, CY, 8, 128), (16, 4, MIG), (16, 4, CORNER)],
         [
-            scratch((2, Y_ROWS, 128)),
             scratch((2, X_ROWS, 128)),
             scratch((2, YY * 8, 128)),
             scratch((3, YP * 8, 128)),
@@ -652,7 +688,7 @@
             pltpu.SemaphoreType.DMA((6,)),
         ],
         10_000_000,
-    )(res, cell_count, joined, y1, y0, x1, x0)
+    )(res, joined, weights, rows, depth, across, x1, x0)
     out = out.reshape(16, CY, 2, CX, 128).transpose(0, 3, 1, 2, 4).reshape(16, CX, CY * 256)
     return out, face_out, corner_out
 

time: 21.2 us -> 20.9 us (0.986)
  waiting for transfers between devices: 5.19 us -> 4.93 us
    ppermute x4, waiting for transfers between devices: 5.19 us -> 4.93 us  [swapped(): lax.ppermute(value, axis, [(i, partner(i, phase, count)) for i in range(c...]
    pallas_call x1 -> x2, Pallas kernels: 2.55 us -> 2.48 us  [the longest x1 2.26 us: body(): call(last_kernel, [VMEM] * 8, HBM, [(16, CY, 8, 128), (16, 4, MIG), (16,...]
  transfers between devices with their start and end apart: 4 -> 4, of which waited for: 3 -> 3; matrix products, arithmetic and copies ran while one was open for 0% -> 0% of each run, Pallas kernels for 7% -> 8%
where the time goes in v4:
time: 20.9 us; the launch traced here: 20.8 us
  starting transfers between devices  8.97 us (43%)
  Pallas kernels  5.35 us (26%)
  waiting for transfers between devices  4.93 us (24%)
  local copies, waits for them, and re-layouts  0.8 us (4%)
  between operations  0.73 us (3%)
    ppermute x4, starting transfers between devices, swapped(): lax.ppermute(value, axis, [(i, partner(i, phase, count)) for i in range(c...  8.97 us
    ppermute x4, waiting for transfers between devices, swapped(): lax.ppermute(value, axis, [(i, partner(i, phase, count)) for i in range(c...  4.93 us
    pallas_call x1, Pallas kernels, body(): call(last_kernel, [VMEM] * 8, HBM, [(16, CY, 8, 128), (16, 4, MIG), (16,...  2.26 us
    pallas_call x1, Pallas kernels, body(): call(inner_kernel, [VMEM] * 4, VMEM, [(2, YY * 8, 128)], [scratch((4, YP...  1.48 us
    unnamed x14, local copies, waits for them, and re-layouts  0.8 us
    pallas_call x1, Pallas kernels, body(): call(leave_kernel, [VMEM] * 6, VMEM, [(4, YP * 8, 128), (2, Y_ROWS - Y_ST...  0.77 us
    pallas_call x1, Pallas kernels, body(): call(edge_kernel, [VMEM] * 4, VMEM, [(Y_ROWS, 128), (Y_ROWS, 128), (4, YP...  0.5 us
  transfers between devices with their start and end apart: 4, of which 3 were waited for; matrix products, arithmetic and copies ran while one was open for 0% of the time, Pallas kernels for 8%

profile of v4, /device:TPU:0, one launch (start us, length us, event | category | flops | bytes accessed | tf_op | source)
XLA Modules:
  0.0 20.8 jit_solution(4031692949649621614)
XLA Ops:
  0.6 0.0 copy-start.3
  0.6 0.0 copy-start.2
  0.7 0.0 copy-start.4
  0.7 0.0 copy-start.5
  0.7 0.0 copy-start
  0.7 0.0 copy-start.1
  0.7 0.0 copy-start.6
  0.7 0.7 %copy-done.3 = f32[16,4,64]{2,1,0:T(4,128)S(1)} copy-done((f32[16,4,64]{2,1,0:T(4,128)S(1)}, f32[16,4,64]{2,1,0:T(4,128)}, u32[]{:S(2)}) %copy-start.3) | copy-done | bytes 16408
  1.4 0.1 copy-done.2
  1.5 0.8 %shard_map.95 = (f32[4,192,128]{2,1,0:T(8,128)S(1)}, f32[2,56,128]{2,1,0:T(8,128)S(1)}, f32[2,40,128]{2,1,0:T(8,128)S(1)}, f32[17,2,384]{2,1,0:T(2,128)S(1)}) custom-call(f32[8,128]{1,0:T(8,128)S(1)} %shard_map.94.mark_ref, s32[1,8]{1,0:T(1,128)S(1)} %bitcast.15, f32[16,4,256]{2,1,0:T(4,128)S(1)} %copy-done.2, f32[16,4,64]{2,1,0:T(4,128)S(1)} %copy-done.3, ...), custom_call_target="tpu_custom_call" | custom-call | flops 10000000 | bytes 1048576 | tf_op jit(solution)/shard_map/pallas_call | solution.py:631
  2.3 0.0 copy-done
  2.3 0.5 %shard_map.96 = (f32[104,128]{1,0:T(8,128)S(1)}, f32[104,128]{1,0:T(8,128)S(1)}, f32[4,192,128]{2,1,0:T(8,128)S(1)}) custom-call(f32[16,16,8,128]{3,2,1,0:T(8,128)S(1)} %bitcast.11, s32[4,1024]{1,0:T(4,128)S(1)} %copy-done.1, f32[2,56,128]{2,1,0:T(8,128)S(1)} %get-tuple-element.20.states_ref, f32[4,192,128]{2,1,0:T(8,128)S(1)} %get-tuple-element.21.before_ref), custom_call_target="tpu_custom_call" | custom-call | flops 10000000 | bytes 1048576 | tf_op jit(solution)/shard_map/pallas_call | solution.py:639
  2.8 3.9 %collective-permute-start = (f32[104,128]{1,0:T(8,128)S(1)}, f32[104,128]{1,0:T(8,128)S(1)}, u32[]{:S(2)}, u32[]{:S(2)}) collective-permute-start(f32[104,128]{1,0:T(8,128)S(1)} %get-tuple-element.24), channel_id=1, source_target_pairs={{0,7},{1,2},{2,1},{3,4},{4,3},{5,6},{6,5},{7,0},{8,15},{9,10},{10,... | collective-permute-start | bytes 159752 | tf_op jit(solution)/shard_map/ppermute | solution.py:602
  6.7 0.0 collective-permute-start.1
  6.7 1.5 %shard_map.97.grid_ref = f32[2,160,128]{2,1,0:T(8,128)S(1)} custom-call(f32[16,16,8,128]{3,2,1,0:T(8,128)S(1)} %bitcast.12, s32[4,1024]{1,0:T(4,128)S(1)} %copy-done.1, f32[4,192,128]{2,1,0:T(8,128)S(1)} %get-tuple-element.22.before_ref, f32[17,2,384]{2,1,0:T(2,128)S(1)} %get-tuple-element.23.wide_ref), custom_call_target="tpu_custom_call" | custom-call | flops 10000000 | bytes 1048576 | tf_op jit(solution)/shard_map/pallas_call | solution.py:649
  8.2 0.9 %collective-permute-done.in1_ref.y1_ref = f32[104,128]{1,0:T(8,128)S(1)} collective-permute-done((f32[104,128]{1,0:T(8,128)S(1)}, f32[104,128]{1,0:T(8,128)S(1)}, u32[]{:S(2)}, u32[]{:S(2)}) %collective-permute-start) | collective-permute-done | bytes 53280 | tf_op jit(solution)/shard_map/ppermute | solution.py:602
  9.1 1.7 %collective-permute-done.1.in0_ref.y0_ref = f32[104,128]{1,0:T(8,128)S(1)} collective-permute-done((f32[104,128]{1,0:T(8,128)S(1)}, f32[104,128]{1,0:T(8,128)S(1)}, u32[]{:S(2)}, u32[]{:S(2)}) %collective-permute-start.1) | collective-permute-done | bytes 53280 | tf_op jit(solution)/shard_map/ppermute | solution.py:602
  10.9 0.1 shard_map.98
  11.0 5.0 %collective-permute-start.2 = (f32[160,128]{1,0:T(8,128)S(1)}, f32[160,128]{1,0:T(8,128)S(1)}, u32[]{:S(2)}, u32[]{:S(2)}) collective-permute-start(f32[160,128]{1,0:T(8,128)S(1)} %get-tuple-element.32), channel_id=1, source_target_pairs={{0,120},{8,16},{16,8},{24,32},{32,24},{40,48},{48,40},{56,64},{64,... | collective-permute-start | bytes 245768 | tf_op jit(solution)/shard_map/ppermute | solution.py:602
  16.0 0.0 collective-permute-start.3
  16.0 0.2 %shard_map.99 = (f32[16,10,8,128]{3,2,1,0:T(8,128)S(1)}, f32[20,2,256]{2,1,0:T(2,128)S(1)}, bf16[2,2,64,512]{3,2,1,0:T(8,128)(2,1)S(1)}, f32[2,2,8,256]{3,2,1,0:T(8,128)S(1)}) custom-call(f32[16,16,8,128]{3,2,1,0:T(8,128)S(1)} %bitcast.13, s32[4,1024]{1,0:T(4,128)S(1)} %copy-done.1, f32[104,128]{1,0:T(8,128)S(1)} %collective-permute-done.in1_ref.y1_ref, ...), custom_call_target="tpu_custom_call" | custom-call | flops 10000000 | bytes 1048576 | tf_op jit(solution)/shard_map/pallas_call | solution.py:667
  16.2 2.3 %collective-permute-done.2.x1_ref = f32[160,128]{1,0:T(8,128)S(1)} collective-permute-done((f32[160,128]{1,0:T(8,128)S(1)}, f32[160,128]{1,0:T(8,128)S(1)}, u32[]{:S(2)}, u32[]{:S(2)}) %collective-permute-start.2) | collective-permute-done | bytes 81952 | tf_op jit(solution)/shard_map/ppermute | solution.py:602
  18.5 0.0 collective-permute-done.3.x0_ref
  18.5 2.3 %shard_map.100 = (f32[16,16,8,128]{3,2,1,0:T(8,128)}, f32[16,4,256]{2,1,0:T(4,128)}, f32[16,4,64]{2,1,0:T(4,128)}) custom-call(f32[16,16,8,128]{3,2,1,0:T(8,128)S(1)} %bitcast.14, f32[2,160,128]{2,1,0:T(8,128)S(1)} %get-tuple-element.27.joined_ref, f32[16,10,8,128]{3,2,1,0:T(8,128)S(1)} %get-tuple-element.28.weights_ref, ...), custom_call_target="tpu_custom_call" | custom-call | flops 10000000 | bytes 1048576 | tf_op jit(solution)/shard_map/pallas_call | solution.py:675
  (5 shorter events, 0.0 us)
Async XLA Ops:
  0.6 0.8 %copy-start.3 = (f32[16,4,64]{2,1,0:T(4,128)S(1)}, f32[16,4,64]{2,1,0:T(4,128)}, u32[]{:S(2)}) copy-start(f32[16,4,64]{2,1,0:T(4,128)} %corner_ref.1) | copy-start | bytes 49156
  0.6 0.8 %copy-start.2 = (f32[16,4,256]{2,1,0:T(4,128)S(1)}, f32[16,4,256]{2,1,0:T(4,128)}, u32[]{:S(2)}) copy-start(f32[16,4,256]{2,1,0:T(4,128)} %outbox_ref.1) | copy-start | bytes 196612
  0.7 0.8 %copy-start.4 = (s32[4,256]{1,0:T(4,128)S(1)}, s32[4,256]{1,0:T(4,128)}, u32[]{:S(2)}) copy-start(s32[4,256]{1,0:T(4,128)} %face_cell_ref.1) | copy-start | bytes 12292
  0.7 0.8 %copy-start.5 = (s32[4,64]{1,0:T(4,128)S(1)}, s32[4,64]{1,0:T(4,128)}, u32[]{:S(2)}) copy-start(s32[4,64]{1,0:T(4,128)} %corner_cell_ref.1) | copy-start | bytes 3076
  0.7 1.6 %copy-start = (f32[16,4,4096]{2,1,0:T(4,128)S(1)}, f32[16,4,4096]{2,1,0:T(4,128)}, u32[]{:S(2)}) copy-start(f32[16,4,4096]{2,1,0:T(4,128)} %param.7) | copy-start | bytes 3145732
  0.7 1.6 %copy-start.1 = (s32[4,1024]{1,0:T(4,128)S(1)}, s32[4,1024]{1,0:T(4,128)}, u32[]{:S(2)}) copy-start(s32[4,1024]{1,0:T(4,128)} %cells_ref.5) | copy-start | bytes 49156
  0.7 0.8 %copy-start.6 = (s32[8,1]{0,1:T(1,128)S(1)}, s32[8,1]{0,1:T(1,128)}, u32[]{:S(2)}) copy-start(s32[8,1]{0,1:T(1,128)} %param.13) | copy-start | bytes 100
  2.8 6.3 %collective-permute-start = (f32[104,128]{1,0:T(8,128)S(1)}, f32[104,128]{1,0:T(8,128)S(1)}, u32[]{:S(2)}, u32[]{:S(2)}) collective-permute-start(f32[104,128]{1,0:T(8,128)S(1)} %get-tuple-element.24), channel_id=1, source_target_pairs={{0,7},{1,2},{2,1},{3,4},{4,3},{5,6},{6,5},{7,0},{8,15},{9,10},{10,... | collective-permute-start | bytes 159752 | tf_op jit(solution)/shard_map/ppermute | solution.py:602
  6.7 4.1 %collective-permute-start.1 = (f32[104,128]{1,0:T(8,128)S(1)}, f32[104,128]{1,0:T(8,128)S(1)}, u32[]{:S(2)}, u32[]{:S(2)}) collective-permute-start(f32[104,128]{1,0:T(8,128)S(1)} %get-tuple-element.25), channel_id=1, source_target_pairs={{0,1},{1,0},{2,3},{3,2},{4,5},{5,4},{6,7},{7,6},{8,9},{9,8},{10,11... | collective-permute-start | bytes 159752 | tf_op jit(solution)/shard_map/ppermute | solution.py:602
  11.0 7.6 %collective-permute-start.2 = (f32[160,128]{1,0:T(8,128)S(1)}, f32[160,128]{1,0:T(8,128)S(1)}, u32[]{:S(2)}, u32[]{:S(2)}) collective-permute-start(f32[160,128]{1,0:T(8,128)S(1)} %get-tuple-element.32), channel_id=1, source_target_pairs={{0,120},{8,16},{16,8},{24,32},{32,24},{40,48},{48,40},{56,64},{64,... | collective-permute-start | bytes 245768 | tf_op jit(solution)/shard_map/ppermute | solution.py:602
  16.0 2.5 %collective-permute-start.3 = (f32[160,128]{1,0:T(8,128)S(1)}, f32[160,128]{1,0:T(8,128)S(1)}, u32[]{:S(2)}, u32[]{:S(2)}) collective-permute-start(f32[160,128]{1,0:T(8,128)S(1)} %get-tuple-element.33), channel_id=1, source_target_pairs={{0,8},{8,0},{16,24},{24,16},{32,40},{40,32},{48,56},{56,48},{64,72... | collective-permute-start | bytes 245768 | tf_op jit(solution)/shard_map/ppermute | solution.py:602

commit v5 on v4

--- a/solution.py
+++ b/solution.py
@@ -54,6 +54,20 @@
     return plain, moment
 
 
+def placed_depth(width, cell, weights):
+    row = lax.broadcasted_iota(jnp.int32, (NZ, width), 0).astype(F32).astype(BF16)
+    step = row - jnp.broadcast_to(cell.astype(F32).astype(BF16), (NZ, width))
+    is_low, is_mid, is_high = step == -1.0, step == 0.0, step == 1.0
+    zero = jnp.zeros((NZ, width), BF16)
+    parts = []
+    for low, mid, high in zip(*[split(value) for value in weights]):
+        low, mid, high = [jnp.broadcast_to(value, (NZ, width)) for value in (low, mid, high)]
+        moment = jnp.where(is_low, -low, jnp.where(is_high, high, zero))
+        plain = jnp.where(is_low, low, jnp.where(is_high, high, jnp.where(is_mid, mid, zero)))
+        parts.append(jnp.concatenate([plain, moment], axis=1))
+    return parts
+
+
 def split(value):
     coarse = value.astype(BF16)
     fine = (value - coarse.astype(F32)).astype(BF16)
@@ -68,9 +82,8 @@
     return pltpu.roll(value, NZ, value.ndim - 1)
 
 
-def scatter_product(lhs, depth_plain, depth_moment):
-    rhs = jnp.concatenate([depth_plain, depth_moment], axis=1)
-    rhs = jnp.concatenate(split(rhs), axis=0)
+def scatter_product(lhs, coarse_depth, fine_depth):
+    rhs = jnp.concatenate([coarse_depth, fine_depth], axis=0)
     rows = lhs.shape[0]
     product = lax.dot_general(
         jnp.concatenate(split(lhs), axis=0), rhs, (((1,), (1,)), ((), ())), preferred_element_type=F32
@@ -190,7 +203,7 @@
         elif row_nodes[k] != row_nodes[k - 1] + 1:
             node = jnp.where(row >= k, row + (row_nodes[k] - k), node)
     for g in range(2):
-        depth = placed(NZ, WIDE, row_of(cell_z, g), [row_of(w, g) for w in weights[2]])
+        depth = placed_depth(WIDE, row_of(cell_z, g), [row_of(w, g) for w in weights[2]])
         across, across_moment = placed(
             rows, WIDE, row_of(cell_y, g), [row_of(w, g) for w in weights[1]], row=node
         )
@@ -280,7 +293,7 @@
     mass, carried, affine = deposit_terms(state, living)
     weights = [spline(state[axis]) for axis in range(3)]
     for g in range(2):
-        depth = placed(NZ, MIG, row_of(cell_z, g), [row_of(w, g) for w in weights[2]])
+        depth = placed_depth(MIG, row_of(cell_z, g), [row_of(w, g) for w in weights[2]])
         across, across_moment = placed(8, MIG, row_of(cell_x, g) + 2, [row_of(w, g) for w in weights[0]])
         lines = []
         zero = jnp.zeros((8, MIG), F32)
@@ -376,10 +389,6 @@
     return jnp.concatenate([first, second], axis=0)
 
 
-def split_depth(depth_plain, depth_moment):
-    return split(jnp.concatenate([depth_plain, depth_moment], axis=1))
-
-
 def gather_product(nodes, coarse_depth, fine_depth):
     low = low_half(nodes.shape)
     coarse = nodes.astype(BF16).astype(F32)
@@ -432,7 +441,7 @@
 def laid_out(side, rows, width, number, across_cell, depth_weights, across_weights):
     depth = placed(NZ, width, row_of(number % NZ, side), [row_of(w, side) for w in depth_weights])
     across = placed(rows, width, row_of(across_cell, side), [row_of(w, side) for w in across_weights])
-    return split_depth(*depth), across
+    return split(jnp.concatenate(depth, axis=1)), across
 
 
 def ready_kernel(res_ref, cells_ref, y1_ref, y0_ref, weights_ref, rows_ref, depth_ref, across_ref, got_ref):

time: 20.9 us -> 20.8 us (level)
  no operation moved by 1% of the time
where the time goes in v5:
time: 20.8 us; the launch traced here: 20.7 us
  starting transfers between devices  8.97 us (43%)
  Pallas kernels  5.25 us (25%)
  waiting for transfers between devices  4.94 us (24%)
  local copies, waits for them, and re-layouts  0.8 us (4%)
  between operations  0.74 us (4%)
    ppermute x4, starting transfers between devices, swapped(): lax.ppermute(value, axis, [(i, partner(i, phase, count)) for i in range(c...  8.97 us
    ppermute x4, waiting for transfers between devices, swapped(): lax.ppermute(value, axis, [(i, partner(i, phase, count)) for i in range(c...  4.94 us
    pallas_call x1, Pallas kernels, body(): call(last_kernel, [VMEM] * 8, HBM, [(16, CY, 8, 128), (16, 4, MIG), (16,...  2.25 us
    pallas_call x1, Pallas kernels, body(): call(inner_kernel, [VMEM] * 4, VMEM, [(2, YY * 8, 128)], [scratch((4, YP...  1.47 us
    unnamed x14, local copies, waits for them, and re-layouts  0.8 us
    pallas_call x1, Pallas kernels, body(): call(leave_kernel, [VMEM] * 6, VMEM, [(4, YP * 8, 128), (2, Y_ROWS - Y_ST...  0.7 us
    pallas_call x1, Pallas kernels, body(): call(edge_kernel, [VMEM] * 4, VMEM, [(Y_ROWS, 128), (Y_ROWS, 128), (4, YP...  0.5 us
  transfers between devices with their start and end apart: 4, of which 3 were waited for; matrix products, arithmetic and copies ran while one was open for 0% of the time, Pallas kernels for 8%

profile of v5, /device:TPU:0, one launch (start us, length us, event | category | flops | bytes accessed | tf_op | source)
XLA Modules:
  0.0 20.7 jit_solution(16518273968941513193)
XLA Ops:
  0.6 0.0 copy-start.3
  0.6 0.0 copy-start.2
  0.7 0.0 copy-start.4
  0.7 0.0 copy-start.5
  0.7 0.0 copy-start
  0.7 0.0 copy-start.1
  0.7 0.0 copy-start.6
  0.7 0.7 %copy-done.3 = f32[16,4,64]{2,1,0:T(4,128)S(1)} copy-done((f32[16,4,64]{2,1,0:T(4,128)S(1)}, f32[16,4,64]{2,1,0:T(4,128)}, u32[]{:S(2)}) %copy-start.3) | copy-done | bytes 16408
  1.4 0.1 copy-done.2
  1.5 0.0 copy-done.4
  1.5 0.7 %shard_map.95 = (f32[4,192,128]{2,1,0:T(8,128)S(1)}, f32[2,56,128]{2,1,0:T(8,128)S(1)}, f32[2,40,128]{2,1,0:T(8,128)S(1)}, f32[17,2,384]{2,1,0:T(2,128)S(1)}) custom-call(f32[8,128]{1,0:T(8,128)S(1)} %shard_map.94.mark_ref, s32[1,8]{1,0:T(1,128)S(1)} %bitcast.15, f32[16,4,256]{2,1,0:T(4,128)S(1)} %copy-done.2, f32[16,4,64]{2,1,0:T(4,128)S(1)} %copy-done.3, ...), custom_call_target="tpu_custom_call" | custom-call | flops 10000000 | bytes 1048576 | tf_op jit(solution)/shard_map/pallas_call | solution.py:640
  2.2 0.5 %shard_map.96 = (f32[104,128]{1,0:T(8,128)S(1)}, f32[104,128]{1,0:T(8,128)S(1)}, f32[4,192,128]{2,1,0:T(8,128)S(1)}) custom-call(f32[16,16,8,128]{3,2,1,0:T(8,128)S(1)} %bitcast.11, s32[4,1024]{1,0:T(4,128)S(1)} %copy-done.1, f32[2,56,128]{2,1,0:T(8,128)S(1)} %get-tuple-element.20.states_ref, f32[4,192,128]{2,1,0:T(8,128)S(1)} %get-tuple-element.21.before_ref), custom_call_target="tpu_custom_call" | custom-call | flops 10000000 | bytes 1048576 | tf_op jit(solution)/shard_map/pallas_call | solution.py:648
  2.7 3.9 %collective-permute-start = (f32[104,128]{1,0:T(8,128)S(1)}, f32[104,128]{1,0:T(8,128)S(1)}, u32[]{:S(2)}, u32[]{:S(2)}) collective-permute-start(f32[104,128]{1,0:T(8,128)S(1)} %get-tuple-element.24), channel_id=1, source_target_pairs={{0,7},{1,2},{2,1},{3,4},{4,3},{5,6},{6,5},{7,0},{8,15},{9,10},{10,... | collective-permute-start | bytes 159752 | tf_op jit(solution)/shard_map/ppermute | solution.py:611
  6.7 0.0 collective-permute-start.1
  6.7 1.5 %shard_map.97.grid_ref = f32[2,160,128]{2,1,0:T(8,128)S(1)} custom-call(f32[16,16,8,128]{3,2,1,0:T(8,128)S(1)} %bitcast.12, s32[4,1024]{1,0:T(4,128)S(1)} %copy-done.1, f32[4,192,128]{2,1,0:T(8,128)S(1)} %get-tuple-element.22.before_ref, f32[17,2,384]{2,1,0:T(2,128)S(1)} %get-tuple-element.23.wide_ref), custom_call_target="tpu_custom_call" | custom-call | flops 10000000 | bytes 1048576 | tf_op jit(solution)/shard_map/pallas_call | solution.py:658
  8.1 0.9 %collective-permute-done.in1_ref.y1_ref = f32[104,128]{1,0:T(8,128)S(1)} collective-permute-done((f32[104,128]{1,0:T(8,128)S(1)}, f32[104,128]{1,0:T(8,128)S(1)}, u32[]{:S(2)}, u32[]{:S(2)}) %collective-permute-start) | collective-permute-done | bytes 53280 | tf_op jit(solution)/shard_map/ppermute | solution.py:611
  9.1 1.7 %collective-permute-done.1.in0_ref.y0_ref = f32[104,128]{1,0:T(8,128)S(1)} collective-permute-done((f32[104,128]{1,0:T(8,128)S(1)}, f32[104,128]{1,0:T(8,128)S(1)}, u32[]{:S(2)}, u32[]{:S(2)}) %collective-permute-start.1) | collective-permute-done | bytes 53280 | tf_op jit(solution)/shard_map/ppermute | solution.py:611
  10.8 0.1 shard_map.98
  10.9 5.0 %collective-permute-start.2 = (f32[160,128]{1,0:T(8,128)S(1)}, f32[160,128]{1,0:T(8,128)S(1)}, u32[]{:S(2)}, u32[]{:S(2)}) collective-permute-start(f32[160,128]{1,0:T(8,128)S(1)} %get-tuple-element.32), channel_id=1, source_target_pairs={{0,120},{8,16},{16,8},{24,32},{32,24},{40,48},{48,40},{56,64},{64,... | collective-permute-start | bytes 245768 | tf_op jit(solution)/shard_map/ppermute | solution.py:611
  15.9 0.0 collective-permute-start.3
  15.9 0.2 %shard_map.99 = (f32[16,10,8,128]{3,2,1,0:T(8,128)S(1)}, f32[20,2,256]{2,1,0:T(2,128)S(1)}, bf16[2,2,64,512]{3,2,1,0:T(8,128)(2,1)S(1)}, f32[2,2,8,256]{3,2,1,0:T(8,128)S(1)}) custom-call(f32[16,16,8,128]{3,2,1,0:T(8,128)S(1)} %bitcast.13, s32[4,1024]{1,0:T(4,128)S(1)} %copy-done.1, f32[104,128]{1,0:T(8,128)S(1)} %collective-permute-done.in1_ref.y1_ref, ...), custom_call_target="tpu_custom_call" | custom-call | flops 10000000 | bytes 1048576 | tf_op jit(solution)/shard_map/pallas_call | solution.py:676
  16.2 2.3 %collective-permute-done.2.x1_ref = f32[160,128]{1,0:T(8,128)S(1)} collective-permute-done((f32[160,128]{1,0:T(8,128)S(1)}, f32[160,128]{1,0:T(8,128)S(1)}, u32[]{:S(2)}, u32[]{:S(2)}) %collective-permute-start.2) | collective-permute-done | bytes 81952 | tf_op jit(solution)/shard_map/ppermute | solution.py:611
  18.5 0.0 collective-permute-done.3.x0_ref
  18.5 2.2 %shard_map.100 = (f32[16,16,8,128]{3,2,1,0:T(8,128)}, f32[16,4,256]{2,1,0:T(4,128)}, f32[16,4,64]{2,1,0:T(4,128)}) custom-call(f32[16,16,8,128]{3,2,1,0:T(8,128)S(1)} %bitcast.14, f32[2,160,128]{2,1,0:T(8,128)S(1)} %get-tuple-element.27.joined_ref, f32[16,10,8,128]{3,2,1,0:T(8,128)S(1)} %get-tuple-element.28.weights_ref, ...), custom_call_target="tpu_custom_call" | custom-call | flops 10000000 | bytes 1048576 | tf_op jit(solution)/shard_map/pallas_call | solution.py:684
  (5 shorter events, 0.0 us)
Async XLA Ops:
  0.6 0.8 %copy-start.3 = (f32[16,4,64]{2,1,0:T(4,128)S(1)}, f32[16,4,64]{2,1,0:T(4,128)}, u32[]{:S(2)}) copy-start(f32[16,4,64]{2,1,0:T(4,128)} %corner_ref.1) | copy-start | bytes 49156
  0.6 0.8 %copy-start.2 = (f32[16,4,256]{2,1,0:T(4,128)S(1)}, f32[16,4,256]{2,1,0:T(4,128)}, u32[]{:S(2)}) copy-start(f32[16,4,256]{2,1,0:T(4,128)} %outbox_ref.1) | copy-start | bytes 196612
  0.7 0.8 %copy-start.4 = (s32[4,256]{1,0:T(4,128)S(1)}, s32[4,256]{1,0:T(4,128)}, u32[]{:S(2)}) copy-start(s32[4,256]{1,0:T(4,128)} %face_cell_ref.1) | copy-start | bytes 12292
  0.7 0.8 %copy-start.5 = (s32[4,64]{1,0:T(4,128)S(1)}, s32[4,64]{1,0:T(4,128)}, u32[]{:S(2)}) copy-start(s32[4,64]{1,0:T(4,128)} %corner_cell_ref.1) | copy-start | bytes 3076
  0.7 1.5 %copy-start = (f32[16,4,4096]{2,1,0:T(4,128)S(1)}, f32[16,4,4096]{2,1,0:T(4,128)}, u32[]{:S(2)}) copy-start(f32[16,4,4096]{2,1,0:T(4,128)} %param.7) | copy-start | bytes 3145732
  0.7 1.5 %copy-start.1 = (s32[4,1024]{1,0:T(4,128)S(1)}, s32[4,1024]{1,0:T(4,128)}, u32[]{:S(2)}) copy-start(s32[4,1024]{1,0:T(4,128)} %cells_ref.5) | copy-start | bytes 49156
  0.7 0.8 %copy-start.6 = (s32[8,1]{0,1:T(1,128)S(1)}, s32[8,1]{0,1:T(1,128)}, u32[]{:S(2)}) copy-start(s32[8,1]{0,1:T(1,128)} %param.13) | copy-start | bytes 100
  2.7 6.3 %collective-permute-start = (f32[104,128]{1,0:T(8,128)S(1)}, f32[104,128]{1,0:T(8,128)S(1)}, u32[]{:S(2)}, u32[]{:S(2)}) collective-permute-start(f32[104,128]{1,0:T(8,128)S(1)} %get-tuple-element.24), channel_id=1, source_target_pairs={{0,7},{1,2},{2,1},{3,4},{4,3},{5,6},{6,5},{7,0},{8,15},{9,10},{10,... | collective-permute-start | bytes 159752 | tf_op jit(solution)/shard_map/ppermute | solution.py:611
  6.7 4.1 %collective-permute-start.1 = (f32[104,128]{1,0:T(8,128)S(1)}, f32[104,128]{1,0:T(8,128)S(1)}, u32[]{:S(2)}, u32[]{:S(2)}) collective-permute-start(f32[104,128]{1,0:T(8,128)S(1)} %get-tuple-element.25), channel_id=1, source_target_pairs={{0,1},{1,0},{2,3},{3,2},{4,5},{5,4},{6,7},{7,6},{8,9},{9,8},{10,11... | collective-permute-start | bytes 159752 | tf_op jit(solution)/shard_map/ppermute | solution.py:611
  10.9 7.6 %collective-permute-start.2 = (f32[160,128]{1,0:T(8,128)S(1)}, f32[160,128]{1,0:T(8,128)S(1)}, u32[]{:S(2)}, u32[]{:S(2)}) collective-permute-start(f32[160,128]{1,0:T(8,128)S(1)} %get-tuple-element.32), channel_id=1, source_target_pairs={{0,120},{8,16},{16,8},{24,32},{32,24},{40,48},{48,40},{56,64},{64,... | collective-permute-start | bytes 245768 | tf_op jit(solution)/shard_map/ppermute | solution.py:611
  15.9 2.5 %collective-permute-start.3 = (f32[160,128]{1,0:T(8,128)S(1)}, f32[160,128]{1,0:T(8,128)S(1)}, u32[]{:S(2)}, u32[]{:S(2)}) collective-permute-start(f32[160,128]{1,0:T(8,128)S(1)} %get-tuple-element.33), channel_id=1, source_target_pairs={{0,8},{8,0},{16,24},{24,16},{32,40},{40,32},{48,56},{56,48},{64,72... | collective-permute-start | bytes 245768 | tf_op jit(solution)/shard_map/ppermute | solution.py:611
